TPU v7x, 512 devices: a whole 4x8x8 slice. The times are simulated.
512 devices in a mesh: rep: 32 (over z_hi, y, core), slab: 16 (over z_lo, x).
Axes of the slice: x: 4, y: 8, z: 8 (z_hi: 2, z_lo: 4; z = z_hi * 4 + z_lo), core: 2. Of those that a mesh axis runs over, the one named last changes fastest.
Arguments:
- phi_field: float32 [32, 64, 256, 256], P('rep', 'slab'), may hold values from -4 to 4
- copy_counts: int32 [32], replicated, may hold values from 0 to 4, as said below
- langevin_noise: float32 [2, 32, 64, 256, 256], P(None, 'rep', 'slab'), may hold values from -6 to 6
Outputs:
- new_field: float32 [32, 64, 256, 256], P('rep', 'slab')
Inputs may be any that keep to these rules, and one draw needn't show every extreme that they name: copy_counts sum to 32; at least one replica has exactly 4 copies, none has more than 4, and some have none.
All inputs are finite; a program needn't handle non-finite values.
Results may differ from a plain program's by a relative error of at most 0.00002.
Values sent between devices are 32-bit elements; how exact they have to be, the bound alone decides.
No kernel may reach another device: no remote copies, remote signals or barrier semaphores. Data moves between devices by JAX's collectives and lax.ppermute only.
A program may use at most 64 MiB of HBM per device.

v0:
```python
import jax
import jax.numpy as jnp
from jax import lax
from jax.sharding import PartitionSpec as P

SWEEPS = 2


STEP_SIZE = 0.05
MASS_TERM = -0.5
COUPLING = 0.5


def with_halo(array, sides, width):
    for axis, dim in sides:
        size, length = (lax.axis_size(axis), array.shape[dim])
        up = [(i, (i + 1) % size) for i in range(size)]
        down = [(j, i) for i, j in up]
        last = lax.slice_in_dim(array, length - width, length, axis=dim)
        initial = lax.slice_in_dim(array, 0, width, axis=dim)
        before = lax.ppermute(last, axis, up)
        after = lax.ppermute(initial, axis, down)
        array = jnp.concatenate([before, array, after], axis=dim)
    return array


def resample_map(copy_counts):
    replica_ids = jnp.arange(copy_counts.shape[0], dtype=jnp.int32)
    extra_copies = jnp.maximum(copy_counts - 1, 0)
    inclusive = jnp.cumsum(extra_copies)
    empty_slot = (copy_counts == 0).astype(jnp.int32)
    gap_rank = jnp.cumsum(empty_slot) - empty_slot
    filled = jnp.sum((inclusive[None, :] <= gap_rank[:, None]).astype(jnp.int32), axis=1)
    return jnp.where(copy_counts >= 1, replica_ids, filled)


def advance(center, neighbor_sum, kicks):
    laplace = neighbor_sum - 6.0 * center
    drift = laplace - MASS_TERM * center - COUPLING * center * center * center
    return center + STEP_SIZE * drift + jnp.sqrt(2.0 * STEP_SIZE) * kicks


def planes_sum(padded):
    center = padded[:, 1:-1]
    neighbor_sum = padded[:, 2:] + padded[:, :-2]
    neighbor_sum = neighbor_sum + jnp.roll(center, -1, 2) + jnp.roll(center, 1, 2)
    neighbor_sum = neighbor_sum + jnp.roll(center, -1, 3) + jnp.roll(center, 1, 3)
    return (center, neighbor_sum)


def shards(phi_field, copy_counts, langevin_noise):
    source_map = resample_map(copy_counts)
    spread = lax.all_to_all(phi_field, "rep", split_axis=2, concat_axis=0, tiled=True)
    chosen = jnp.take(spread, source_map, axis=0)
    current = lax.all_to_all(chosen, "rep", split_axis=0, concat_axis=2, tiled=True)
    for sweep_index in range(SWEEPS):
        padded = with_halo(current, (("slab", 1),), 1)
        center, neighbor_sum = planes_sum(padded)
        current = advance(center, neighbor_sum, langevin_noise[sweep_index])
    return current


def solution(mesh):
    return jax.shard_map(
        shards,
        mesh=mesh,
        in_specs=(P("rep", "slab", None, None), P(), P(None, "rep", "slab", None, None)),
        out_specs=P("rep", "slab", None, None),
        check_vma=False,
    )
```

profile of v0, /device:TPU:8, one launch (start us, length us, event | category | flops | bytes accessed | tf_op | source)
XLA Modules:
  0.0 127.6 jit_solution(13469873399913017847)
XLA Ops:
  0.0 2.9 %copy.20 = f32[1,4,256,256]{3,1,0,2:T(4,128)} copy(f32[1,4,256,256]{3,2,1,0:T(8,128)} %param.3) | data formatting | bytes 2097152 | tf_op args[0]
  2.9 16.1 %all-to-all-start = ((f32[1,4,256,256]{3,1,0,2:T(4,128)}), f32[1,4,256,256]{3,1,0,2:T(4,128)S(1)}, u32[]{:S(2)}, u32[]{:S(2)}) async-start(f32[1,4,256,256]{3,1,0,2:T(4,128)} %copy.20), calls=%async_computation | async-start | bytes 2097152 | tf_op jit(solution)/shard_map/all_to_all | solution.py:53
  19.1 0.1 copy.19
  19.2 0.1 reduce-window.18
  19.2 0.1 reduce.1
  19.3 0.1 copy.18
  19.4 0.1 reduce-window.17
  19.5 0.1 reduce
  19.6 0.2 convert_reduce_fusion
  19.8 32.5 %all-to-all-done = f32[1,4,256,256]{3,1,0,2:T(4,128)S(1)} async-done(((f32[1,4,256,256]{3,1,0,2:T(4,128)}), f32[1,4,256,256]{3,1,0,2:T(4,128)S(1)}, u32[]{:S(2)}, u32[]{:S(2)}) %all-to-all-start) | async-done | bytes 1048608 | tf_op jit(solution)/shard_map/all_to_all | solution.py:53
  52.3 0.2 copy.28
  52.5 0.6 gather_fusion
  53.1 0.1 broadcast_select_fusion
  53.3 36.5 %all_to_all.36 = f32[32,4,8,256]{3,2,1,0:T(8,128)S(1)} all-to-all(f32[32,4,8,256]{3,2,1,0:T(8,128)S(1)} %broadcast_select_fusion), channel_id=1, replica_groups=mesh['rep'=32,'slab'=16] {'rep'}, dimensions={0} | all-to-all | bytes 2097152 | tf_op jit(solution)/shard_map/all_to_all | solution.py:55
  89.8 0.1 copy_bitcast_fusion.1
  89.9 0.2 fusion.32
  90.1 0.4 fusion.30
  90.5 0.0 copy-start
  90.5 6.8 %collective-permute-start = (f32[1,1,256,256]{3,2,1,0:T(8,128)S(1)}, f32[1,1,256,256]{3,2,1,0:T(8,128)S(1)}, u32[]{:S(2)}, u32[]{:S(2)}) collective-permute-start(f32[1,1,256,256]{3,2,1,0:T(8,128)S(1)} %get-tuple-element.25), channel_id=1, source_target_pairs={{1,0},{2,1},{3,2},{4,3},{5,4},{6,5},{7,6},{8,7},{9,8},{10,9},{11,1... | collective-permute-start | bytes 786440 | tf_op jit(solution)/shard_map/ppermute | solution.py:22
  97.3 1.9 %collective-permute-start.1 = (f32[1,1,256,256]{3,2,1,0:T(8,128)S(1)}, f32[1,1,256,256]{3,2,1,0:T(8,128)S(1)}, u32[]{:S(2)}, u32[]{:S(2)}) collective-permute-start(f32[1,1,256,256]{3,2,1,0:T(8,128)S(1)} %get-tuple-element.26), channel_id=1, source_target_pairs={{0,1},{1,2},{2,3},{3,4},{4,5},{5,6},{6,7},{7,8},{8,9},{9,10},{10,1... | collective-permute-start | bytes 786440 | tf_op jit(solution)/shard_map/ppermute | solution.py:21
  99.2 0.2 fusion.29
  99.4 2.7 %collective-permute-done = f32[1,1,256,256]{3,2,1,0:T(8,128)S(1)} collective-permute-done((f32[1,1,256,256]{3,2,1,0:T(8,128)S(1)}, f32[1,1,256,256]{3,2,1,0:T(8,128)S(1)}, u32[]{:S(2)}, u32[]{:S(2)}) %collective-permute-start) | collective-permute-done | bytes 262176 | tf_op jit(solution)/shard_map/ppermute | solution.py:22
  102.1 8.0 %collective-permute-done.1 = f32[1,1,256,256]{3,2,1,0:T(8,128)S(1)} collective-permute-done((f32[1,1,256,256]{3,2,1,0:T(8,128)S(1)}, f32[1,1,256,256]{3,2,1,0:T(8,128)S(1)}, u32[]{:S(2)}, u32[]{:S(2)}) %collective-permute-start.1) | collective-permute-done | bytes 262176 | tf_op jit(solution)/shard_map/ppermute | solution.py:21
  110.1 0.9 fusion.3
  111.1 0.2 fusion.27
  111.3 0.4 fusion.25
  111.6 1.9 %collective-permute-start.2 = (f32[1,1,256,256]{3,2,1,0:T(8,128)S(1)}, f32[1,1,256,256]{3,2,1,0:T(8,128)S(1)}, u32[]{:S(2)}, u32[]{:S(2)}) collective-permute-start(f32[1,1,256,256]{3,2,1,0:T(8,128)S(1)} %get-tuple-element.15), channel_id=1, source_target_pairs={{1,0},{2,1},{3,2},{4,3},{5,4},{6,5},{7,6},{8,7},{9,8},{10,9},{11,1... | collective-permute-start | bytes 786440 | tf_op jit(solution)/shard_map/ppermute | solution.py:22
  113.6 3.9 %collective-permute-start.3 = (f32[1,1,256,256]{3,2,1,0:T(8,128)S(1)}, f32[1,1,256,256]{3,2,1,0:T(8,128)S(1)}, u32[]{:S(2)}, u32[]{:S(2)}) collective-permute-start(f32[1,1,256,256]{3,2,1,0:T(8,128)S(1)} %get-tuple-element.16), channel_id=1, source_target_pairs={{0,1},{1,2},{2,3},{3,4},{4,5},{5,6},{6,7},{7,8},{8,9},{9,10},{10,1... | collective-permute-start | bytes 786440 | tf_op jit(solution)/shard_map/ppermute | solution.py:21
  117.5 0.2 fusion.24
  117.7 2.2 %collective-permute-done.2 = f32[1,1,256,256]{3,2,1,0:T(8,128)S(1)} collective-permute-done((f32[1,1,256,256]{3,2,1,0:T(8,128)S(1)}, f32[1,1,256,256]{3,2,1,0:T(8,128)S(1)}, u32[]{:S(2)}, u32[]{:S(2)}) %collective-permute-start.2) | collective-permute-done | bytes 262176 | tf_op jit(solution)/shard_map/ppermute | solution.py:22
  119.9 5.8 %collective-permute-done.3 = f32[1,1,256,256]{3,2,1,0:T(8,128)S(1)} collective-permute-done((f32[1,1,256,256]{3,2,1,0:T(8,128)S(1)}, f32[1,1,256,256]{3,2,1,0:T(8,128)S(1)}, u32[]{:S(2)}, u32[]{:S(2)}) %collective-permute-start.3) | collective-permute-done | bytes 262176 | tf_op jit(solution)/shard_map/ppermute | solution.py:21
  125.7 1.8 %fusion.7 = f32[1,4,256,256]{3,2,1,0:T(8,128)} fusion(f32[1,4,256,256]{3,2,1,0:T(8,128)S(1)} %fusion.3, f32[1,1,256,256]{3,2,1,0:T(8,128)S(1)} %collective-permute-done.3, f32[1,1,256,256]{3,2,1,0:T(8,128)S(1)} %collective-permute-done.2, f32[1,4,1,256]{3,2,1,0:T(1,128)S(1)} %get-tuple-element.12, f32[1,4,255,256]{3,2,1,0:T(8,128)S(1)} %get-tuple-element.14, ...), kind=kLoop, calls=%fused_computation.10 | loop fusion | flops 6029312 | bytes 7864320 | tf_op jit(solution)/shard_map/add | solution.py:40
  (11 shorter events, 0.1 us)
Async XLA Ops:
  0.0 19.0 %copy-start.1 = (s32[32]{0:T(128)S(1)}, s32[32]{0:T(128)}, u32[]{:S(2)}) copy-start(s32[32]{0:T(128)} %param.4) | copy-start | bytes 388
  2.9 49.4 %all-to-all-start = ((f32[1,4,256,256]{3,1,0,2:T(4,128)}), f32[1,4,256,256]{3,1,0,2:T(4,128)S(1)}, u32[]{:S(2)}, u32[]{:S(2)}) async-start(f32[1,4,256,256]{3,1,0,2:T(4,128)} %copy.20), calls=%async_computation | async-start | bytes 2097152 | tf_op jit(solution)/shard_map/all_to_all | solution.py:53
  90.5 19.7 %copy-start = (f32[2,1,4,256,256]{4,3,2,1,0:T(8,128)S(1)}, f32[2,1,4,256,256]{4,3,2,1,0:T(8,128)}, u32[]{:S(2)}) copy-start(f32[2,1,4,256,256]{4,3,2,1,0:T(8,128)} %param.5) | copy-start | bytes 6291460
  90.5 11.6 %collective-permute-start = (f32[1,1,256,256]{3,2,1,0:T(8,128)S(1)}, f32[1,1,256,256]{3,2,1,0:T(8,128)S(1)}, u32[]{:S(2)}, u32[]{:S(2)}) collective-permute-start(f32[1,1,256,256]{3,2,1,0:T(8,128)S(1)} %get-tuple-element.25), channel_id=1, source_target_pairs={{1,0},{2,1},{3,2},{4,3},{5,4},{6,5},{7,6},{8,7},{9,8},{10,9},{11,1... | collective-permute-start | bytes 786440 | tf_op jit(solution)/shard_map/ppermute | solution.py:22
  97.3 12.8 %collective-permute-start.1 = (f32[1,1,256,256]{3,2,1,0:T(8,128)S(1)}, f32[1,1,256,256]{3,2,1,0:T(8,128)S(1)}, u32[]{:S(2)}, u32[]{:S(2)}) collective-permute-start(f32[1,1,256,256]{3,2,1,0:T(8,128)S(1)} %get-tuple-element.26), channel_id=1, source_target_pairs={{0,1},{1,2},{2,3},{3,4},{4,5},{5,6},{6,7},{7,8},{8,9},{9,10},{10,1... | collective-permute-start | bytes 786440 | tf_op jit(solution)/shard_map/ppermute | solution.py:21
  111.6 8.3 %collective-permute-start.2 = (f32[1,1,256,256]{3,2,1,0:T(8,128)S(1)}, f32[1,1,256,256]{3,2,1,0:T(8,128)S(1)}, u32[]{:S(2)}, u32[]{:S(2)}) collective-permute-start(f32[1,1,256,256]{3,2,1,0:T(8,128)S(1)} %get-tuple-element.15), channel_id=1, source_target_pairs={{1,0},{2,1},{3,2},{4,3},{5,4},{6,5},{7,6},{8,7},{9,8},{10,9},{11,1... | collective-permute-start | bytes 786440 | tf_op jit(solution)/shard_map/ppermute | solution.py:22
  113.6 12.2 %collective-permute-start.3 = (f32[1,1,256,256]{3,2,1,0:T(8,128)S(1)}, f32[1,1,256,256]{3,2,1,0:T(8,128)S(1)}, u32[]{:S(2)}, u32[]{:S(2)}) collective-permute-start(f32[1,1,256,256]{3,2,1,0:T(8,128)S(1)} %get-tuple-element.16), channel_id=1, source_target_pairs={{0,1},{1,2},{2,3},{3,4},{4,5},{5,6},{6,7},{7,8},{8,9},{9,10},{10,1... | collective-permute-start | bytes 786440 | tf_op jit(solution)/shard_map/ppermute | solution.py:21
where the time goes:
time: 128 us
  waiting for transfers between devices  51.2 us (40%)
  blocking collectives  36.5 us (29%)
  starting transfers between devices  30.8 us (24%)
  local copies, waits for them, and re-layouts  5.53 us (4%)
  other arithmetic  3.42 us (3%)
    all_to_all x1, blocking collectives, shards(): lax.all_to_all(chosen, 'rep', split_axis=0, concat_axis=2, tiled=True)  36.5 us
    all_to_all x1, waiting for transfers between devices, shards(): lax.all_to_all(phi_field, 'rep', split_axis=2, concat_axis=0, tiled=True)  32.5 us
    all_to_all x1, starting transfers between devices, shards(): lax.all_to_all(phi_field, 'rep', split_axis=2, concat_axis=0, tiled=True)  16.1 us
    ppermute x2, waiting for transfers between devices, with_halo(): before = lax.ppermute(last, axis, up)  13.9 us
    ppermute x2, starting transfers between devices, with_halo(): after = lax.ppermute(initial, axis, down)  8.76 us
    ppermute x2, starting transfers between devices, with_halo(): before = lax.ppermute(last, axis, up)  5.84 us
    ppermute x2, waiting for transfers between devices, with_halo(): after = lax.ppermute(initial, axis, down)  4.87 us
    unnamed x5, local copies, waits for them, and re-layouts  2.89 us
  transfers between devices with their start and end apart: 5, of which 5 were waited for; matrix products, arithmetic and copies ran while one was open for 1% of the time, Pallas kernels for 0%

commit v1 on v0

v1 whole, which is shorter than its diff:
```python
import functools

import jax
import jax.numpy as jnp
from jax import lax
from jax.experimental import pallas as pl
from jax.experimental.pallas import tpu as pltpu
from jax.sharding import PartitionSpec as P

STEP_SIZE = 0.05
MASS_TERM = -0.5
COUPLING = 0.5
KICK = (2.0 * STEP_SIZE) ** 0.5
HALF = 16
STRIP = 32
VMEM = pl.BlockSpec(memory_space=pltpu.VMEM)
SMEM = pl.BlockSpec(memory_space=pltpu.SMEM)
PARAMS = pltpu.CompilerParams(vmem_limit_bytes=10 * 1024 * 1024)


def cost(flops, size):
    return pl.CostEstimate(flops=flops, bytes_accessed=size, transcendentals=0)


def ring_order():
    return [((3 * y) % 8) * 2 + core for y in range(8) for core in range(2)]


def exchange(parts, order):
    groups = [[half * HALF + i for i in order] for half in range(2)]
    return lax.all_to_all(parts, "rep", split_axis=0, concat_axis=0, tiled=True, axis_index_groups=groups)


def resample_map(copy_counts):
    ids = jnp.arange(copy_counts.shape[0], dtype=jnp.int32)
    upto = ids[None, :] <= ids[:, None]
    extra = jnp.maximum(copy_counts - 1, 0)
    inclusive = jnp.sum(jnp.where(upto, extra[None, :], 0), axis=1)
    empty = (copy_counts == 0).astype(jnp.int32)
    rank = jnp.sum(jnp.where(upto, empty[None, :], 0), axis=1) - empty
    filled = jnp.sum((inclusive[None, :] <= rank[:, None]).astype(jnp.int32), axis=1)
    return jnp.where(copy_counts >= 1, ids, filled)


def routes(copy_counts, order):
    ids = jnp.arange(2 * HALF, dtype=jnp.int32)
    half = lax.axis_index("rep") // HALF
    place = jnp.array([order.index(i) for i in range(HALF)] * 2, jnp.int32)
    source_map = resample_map(copy_counts)
    crosses = source_map // HALF != ids // HALF
    asked = source_map[:, None] == ids[None, :]
    wanted = jnp.any(crosses[:, None] & asked, axis=0)
    count = jnp.sum(wanted.astype(jnp.int32))
    earlier = (ids[None, :] < ids[:, None]) & wanted[None, :]
    rank = jnp.sum(earlier.astype(jnp.int32), axis=1)
    mine = wanted & (ids // HALF == half)
    send = jnp.sum(jnp.where(mine[None, :] & (rank[None, :] == ids[:HALF, None]), place[None, :], 0), axis=1)
    target = jnp.array(order, jnp.int32) + half * HALF
    where_from = jnp.where(ids // HALF == half, place, HALF + rank)
    source = jnp.sum(jnp.where(target[:, None] == ids[None, :], source_map[None, :], 0), axis=1)
    pick = jnp.sum(jnp.where(source[:, None] == ids[None, :], where_from[None, :], 0), axis=1)
    return pick, send, count


def chosen_parts(spread, pick, send, count):
    swap = [(i, (i + HALF) % (2 * HALF)) for i in range(2 * HALF)]

    def crossing(width, spread, pick, send):
        if width == 0:
            return jnp.take(spread, pick, axis=0, mode="clip")
        far = lax.ppermute(jnp.take(spread, send[:width], axis=0, mode="clip"), "rep", swap)
        return jnp.take(jnp.concatenate([spread, far]), pick, axis=0, mode="clip")

    widths = (0, 1, 2, 4, HALF)
    case = sum((count > w).astype(jnp.int32) for w in widths[:-1])
    return lax.switch(case, [functools.partial(crossing, w) for w in widths], spread, pick, send)


def step(ref, plane, start, along_z, kicks):
    rows = lambda first, size: ref[plane, pl.ds(pl.multiple_of(first, 8), size), :]
    center = rows(start, STRIP)
    block = jnp.concatenate([rows((start + 248) % 256, 8), center, rows((start + STRIP) % 256, 8)])
    above = pltpu.roll(block, STRIP + 15, 0)[8 : 8 + STRIP]
    below = pltpu.roll(block, 1, 0)[8 : 8 + STRIP]
    right, left = pltpu.roll(center, 255, 1), pltpu.roll(center, 1, 1)
    laplace = along_z + above + below + right + left - 6.0 * center
    drift = laplace - MASS_TERM * center - COUPLING * center * center * center
    return center + STEP_SIZE * drift + kicks


def strips(body):
    @pl.loop(0, 256 // STRIP)
    def _(i):
        start = pl.multiple_of(i * STRIP, STRIP)
        body(start, pl.ds(start, STRIP))


def edge_kernel(even, field, noise, edge, inner, outer):
    def body(start, here):
        edge[0, here, :] = step(field, 0, start, field[1, here, :], KICK * noise[0, 0, here, :])
        edge[1, here, :] = step(field, 3, start, field[2, here, :], KICK * noise[0, 3, here, :])

    strips(body)

    def fill(below, above):
        below[0] = field[0]
        below[1] = edge[0]
        above[0] = field[3]
        above[1] = edge[1]

    @pl.when(even[0] == 1)
    def _():
        fill(outer, inner)

    @pl.when(even[0] == 0)
    def _():
        fill(inner, outer)


def late_kernel(even, field, edge, first, second, middle, later, last, out, sides):
    def near(below, above):
        def body(start, here):
            sides[0, here, :] = below[1, here, :] + STEP_SIZE * field[0, here, :] + middle[0, here, :]
            sides[3, here, :] = above[1, here, :] + STEP_SIZE * field[3, here, :] + middle[1, here, :]
            low = edge[0, here, :] + STEP_SIZE * below[0, here, :]
            high = edge[1, here, :] + STEP_SIZE * above[0, here, :]
            sides[1, here, :] = low
            sides[2, here, :] = high
            out[1, here, :] = later[0, here, :] + STEP_SIZE * low
            out[2, here, :] = later[1, here, :] + STEP_SIZE * high

        strips(body)

    @pl.when(even[0] == 1)
    def _():
        near(second, first)

    @pl.when(even[0] == 0)
    def _():
        near(first, second)

    def end(start, here):
        out[0, here, :] = step(sides, 1, start, sides[0, here, :], last[0, here, :])
        out[3, here, :] = step(sides, 2, start, sides[3, here, :], last[1, here, :])

    strips(end)


def swept(center, along_z, kicks):
    total = along_z + jnp.roll(center, -1, 1) + jnp.roll(center, 1, 1)
    total = total + jnp.roll(center, -1, 2) + jnp.roll(center, 1, 2)
    laplace = total - 6.0 * center
    drift = laplace - MASS_TERM * center - COUPLING * center * center * center
    return center + STEP_SIZE * drift + KICK * kicks


def shards(phi_field, copy_counts, langevin_noise):
    planes, height, width = phi_field.shape[1:]
    size = lax.axis_size("slab")
    order = ring_order()
    noise = langevin_noise[:, 0]
    spread = exchange(phi_field.reshape(HALF, -1, width), order)
    route = routes(copy_counts, order)
    field = exchange(chosen_parts(spread, *route), order).reshape(planes, height, width)
    even = (lax.axis_index("slab") % 2 == 0).astype(jnp.int32).reshape(1)
    pair = jax.ShapeDtypeStruct((2, height, width), jnp.float32)
    plane = 4 * height * width
    edge, inner, outer = pl.pallas_call(
        edge_kernel,
        out_shape=[pair] * 3,
        in_specs=[SMEM] + [VMEM] * 2,
        out_specs=[VMEM] * 3,
        compiler_params=PARAMS,
        cost_estimate=cost(2 * 16 * plane // 4, 12 * plane),
    )(even, field, noise)
    inner, outer, field = lax.optimization_barrier((inner, outer, field))
    first = lax.ppermute(inner, "slab", [(i, i ^ 1) for i in range(size)])
    second = lax.ppermute(outer, "slab", [(i, (i - 1 + 2 * (i % 2)) % size) for i in range(size)])
    middle = swept(field[1:3], field[2:4] + field[0:2], noise[0, 1:3])
    later = swept(middle, middle[::-1], noise[1, 1:3])
    last = KICK * jnp.concatenate([noise[1, :1], noise[1, 3:]])
    out = pl.pallas_call(
        late_kernel,
        out_shape=jax.ShapeDtypeStruct((planes, height, width), jnp.float32),
        in_specs=[SMEM] + [VMEM] * 7,
        out_specs=VMEM,
        scratch_shapes=[pltpu.VMEM((4, height, width), jnp.float32)],
        compiler_params=PARAMS,
        cost_estimate=cost(3 * 16 * plane // 4, 20 * plane),
    )(even, field, edge, first, second, middle, later, last)
    return out[None]


def solution(mesh):
    return jax.shard_map(
        shards,
        mesh=mesh,
        in_specs=(P("rep", "slab", None, None), P(), P(None, "rep", "slab", None, None)),
        out_specs=P("rep", "slab", None, None),
        check_vma=False,
    )
```

time: 128 us -> 113 us (0.88)
  blocking collectives: 36.5 us -> 0 us
  waiting for transfers between devices: 51.2 us -> 66.6 us
  Pallas kernels: 0 us -> 3.16 us
  between operations: 0.18 us -> 2.77 us
  starting transfers between devices: 30.8 us -> 32.4 us
    all_to_all x1 -> x0, blocking collectives: 36.5 us -> none  [shards(): lax.all_to_all(chosen, 'rep', split_axis=0, concat_axis=2, tiled=True)]
    all_to_all x1 -> x2, waiting for transfers between devices: 32.5 us -> 48.6 us  [exchange(): lax.all_to_all(parts, 'rep', split_axis=0, concat_axis=0, tiled=True, axi...]
    ppermute x4 -> x3, starting transfers between devices: 14.6 us -> 18.6 us  [the longest x1 8.94 us: crossing(): lax.ppermute(jnp.take(spread, send[:width], axis=0, mode='clip'), 'rep',...]
    pallas_call x0 -> x2, Pallas kernels: none -> 3.16 us  [the longest x1 2.16 us: shards(): pl.pallas_call(late_kernel, out_shape=jax.ShapeDtypeStruct((planes, heigh...]
    all_to_all x1 -> x2, starting transfers between devices: 16.1 us -> 13.8 us  [exchange(): lax.all_to_all(parts, 'rep', split_axis=0, concat_axis=0, tiled=True, axi...]
    unnamed x5 -> x10, local copies, waits for them, and re-layouts: 2.89 us -> 0.75 us
    add x2 -> x3, other arithmetic: 2.73 us -> 0.98 us  [the longest x2 0.97 us: swept(): return center + STEP_SIZE * drift + KICK * kicks]
    reduce_sum x1 -> x8, other arithmetic: 0.18 us -> 1.71 us  [the longest x1 0.64 us: routes(): count = jnp.sum(wanted.astype(jnp.int32))]
  transfers between devices with their start and end apart: 5 -> 5, of which waited for: 5 -> 5; matrix products, arithmetic and copies ran while one was open for 1% -> 3% of each run, Pallas kernels for 0% -> 0%
where the time goes in v1:
time: 113 us; the launch traced here: 112 us
  waiting for transfers between devices  66.6 us (59%)
  starting transfers between devices  32.4 us (29%)
  local copies, waits for them, and re-layouts  4.46 us (4%)
  Pallas kernels  3.16 us (3%)
  other arithmetic  2.94 us (3%)
  between operations  2.77 us (2%)
    all_to_all x2, waiting for transfers between devices, exchange(): lax.all_to_all(parts, 'rep', split_axis=0, concat_axis=0, tiled=True, axi...  48.6 us
    all_to_all x2, starting transfers between devices, exchange(): lax.all_to_all(parts, 'rep', split_axis=0, concat_axis=0, tiled=True, axi...  13.8 us
    ppermute x1, starting transfers between devices, crossing(): lax.ppermute(jnp.take(spread, send[:width], axis=0, mode='clip'), 'rep',...  8.94 us
    ppermute x1, waiting for transfers between devices, shards(): lax.ppermute(outer, 'slab', [(i, (i - 1 + 2 * (i % 2)) % size) for i in r...  7.39 us
    ppermute x1, starting transfers between devices, shards(): lax.ppermute(outer, 'slab', [(i, (i - 1 + 2 * (i % 2)) % size) for i in r...  6.28 us
    ppermute x1, waiting for transfers between devices, shards(): first = lax.ppermute(inner, 'slab', [(i, i ^ 1) for i in range(size)])  6.26 us
    ppermute x1, waiting for transfers between devices, crossing(): lax.ppermute(jnp.take(spread, send[:width], axis=0, mode='clip'), 'rep',...  4.42 us
    ppermute x1, starting transfers between devices, shards(): first = lax.ppermute(inner, 'slab', [(i, i ^ 1) for i in range(size)])  3.4 us
  transfers between devices with their start and end apart: 5, of which 5 were waited for; matrix products, arithmetic and copies ran while one was open for 3% of the time, Pallas kernels for 0%

profile of v1, /device:TPU:8, one launch (start us, length us, event | category | flops | bytes accessed | tf_op | source)
XLA Modules:
  0.0 112.4 jit_solution(13399874784995828194)
XLA Ops:
  0.0 9.4 %all-to-all-start = ((f32[16,64,256]{2,1,0:T(8,128)}), f32[16,64,256]{2,1,0:T(8,128)S(1)}, u32[]{:S(2)}, u32[]{:S(2)}) async-start(f32[16,64,256]{2,1,0:T(8,128)} %bitcast.36), calls=%async_computation | async-start | bytes 2097152 | tf_op jit(solution)/shard_map/all_to_all | solution.py:31
  9.5 0.1 select_reduce_fusion.4
  9.6 0.1 select_reduce_fusion.5
  9.7 0.2 convert_reduce_fusion.1
  10.0 0.6 convert_reduce_fusion.2
  13.3 0.1 convert_reduce_fusion
  13.4 0.2 select_reduce_fusion.7
  13.6 0.2 select_reduce_fusion.6
  13.8 22.5 %all-to-all-done = f32[16,64,256]{2,1,0:T(8,128)S(1)} async-done(((f32[16,64,256]{2,1,0:T(8,128)}), f32[16,64,256]{2,1,0:T(8,128)S(1)}, u32[]{:S(2)}, u32[]{:S(2)}) %all-to-all-start) | async-done | bytes 1048608 | tf_op jit(solution)/shard_map/all_to_all | solution.py:31
  36.3 15.8 %conditional.1 = (f32[16,64,256]{2,1,0:T(8,128)}) conditional(s32[]{:T(128)} %clamp.3, (s32[16]{0:T(128)S(1)}, f32[16,64,256]{2,1,0:T(8,128)S(1)}) %tuple.21, (pred[32]{0:T(512)(128)(4,1)S(1)}, f32[16,64,256]{2,1,0:T(8,128)S(1)}, s32[16]{0:T(128)S(1)}, s32[]{:T(128)}, s32[32]{0:T(128)S(1)}, ...), branch_computations={%region_9.10_spmd, %region_10.11_spmd, %region_11.12_spmd, %region... | conditional | flops 528400 | bytes 12593972 | solution.py:76
  36.3 0.2 select_reduce_fusion.1
  36.5 0.6 gather_fusion.2
  37.0 8.9 %collective-permute-start.1 = (f32[2,64,256]{2,1,0:T(8,128)S(1)}, f32[2,64,256]{2,1,0:T(8,128)S(1)}, u32[]{:S(2)}, u32[]{:S(2)}) collective-permute-start(f32[2,64,256]{2,1,0:T(8,128)S(1)} %gather_fusion.2), channel_id=1, source_target_pairs={{0,256},{16,272},{32,288},{48,304},{64,320},{80,336},{96,352},{112... | collective-permute-start | bytes 393224 | tf_op jit(solution)/shard_map/cond/branch_2_fun/ppermute | solution.py:71
  46.0 4.4 %collective-permute-done.1 = f32[2,64,256]{2,1,0:T(8,128)S(1)} collective-permute-done((f32[2,64,256]{2,1,0:T(8,128)S(1)}, f32[2,64,256]{2,1,0:T(8,128)S(1)}, u32[]{:S(2)}, u32[]{:S(2)}) %collective-permute-start.1) | collective-permute-done | bytes 131104 | tf_op jit(solution)/shard_map/cond/branch_2_fun/ppermute | solution.py:71
  50.4 0.1 pad_maximum_fusion.1
  50.5 1.6 %gather_fusion.3 = f32[16,64,256]{2,1,0:T(8,128)} fusion(f32[18,64,256]{2,1,0:T(8,128)S(1)} %pad_maximum_fusion.1, s32[1024]{0:T(1024)S(1)} %pad_clamp_fusion.2), kind=kCustom, calls=%fused_computation.3 | custom fusion | bytes 2097216 | tf_op jit(solution)/shard_map/cond/branch_2_fun/jit(_take)/gather | solution.py:72
  52.1 4.4 %all-to-all-start.1 = ((f32[16,64,256]{2,1,0:T(8,128)}), f32[16,64,256]{2,1,0:T(8,128)S(1)}, u32[]{:S(2)}, u32[]{:S(2)}) async-start(f32[16,64,256]{2,1,0:T(8,128)} %get-tuple-element.164), calls=%async_computation.1 | async-start | bytes 2097152 | tf_op jit(solution)/shard_map/all_to_all | solution.py:31
  56.5 0.7 slice_bitcast_fusion.1
  57.2 26.1 %all-to-all-done.1 = f32[16,64,256]{2,1,0:T(8,128)S(1)} async-done(((f32[16,64,256]{2,1,0:T(8,128)}), f32[16,64,256]{2,1,0:T(8,128)S(1)}, u32[]{:S(2)}, u32[]{:S(2)}) %all-to-all-start.1) | async-done | bytes 1048608 | tf_op jit(solution)/shard_map/all_to_all | solution.py:31
  83.3 1.0 shard_map.55
  84.3 0.1 fusion.25
  84.5 0.2 fusion.26
  84.7 0.7 copy-done.1
  85.5 0.5 fusion.3
  86.0 0.1 fusion.29
  86.1 0.2 fusion.30
  86.3 3.4 %collective-permute-start.4 = (f32[2,256,256]{2,1,0:T(8,128)S(1)}, f32[2,256,256]{2,1,0:T(8,128)S(1)}, u32[]{:S(2)}, u32[]{:S(2)}) collective-permute-start(f32[2,256,256]{2,1,0:T(8,128)S(1)} %get-tuple-element.63), channel_id=1, source_target_pairs={{0,1},{1,0},{2,3},{3,2},{4,5},{5,4},{6,7},{7,6},{8,9},{9,8},{10,11... | collective-permute-start | bytes 1572872 | tf_op jit(solution)/shard_map/ppermute | solution.py:177
  89.8 6.3 %collective-permute-start.5 = (f32[2,256,256]{2,1,0:T(8,128)S(1)}, f32[2,256,256]{2,1,0:T(8,128)S(1)}, u32[]{:S(2)}, u32[]{:S(2)}) collective-permute-start(f32[2,256,256]{2,1,0:T(8,128)S(1)} %get-tuple-element.64), channel_id=1, source_target_pairs={{0,15},{1,2},{2,1},{3,4},{4,3},{5,6},{6,5},{7,8},{8,7},{9,10},{10,... | collective-permute-start | bytes 1572872 | tf_op jit(solution)/shard_map/ppermute | solution.py:178
  96.1 0.5 fusion.7.later
  96.6 6.3 %collective-permute-done.4.first = f32[2,256,256]{2,1,0:T(8,128)S(1)} collective-permute-done((f32[2,256,256]{2,1,0:T(8,128)S(1)}, f32[2,256,256]{2,1,0:T(8,128)S(1)}, u32[]{:S(2)}, u32[]{:S(2)}) %collective-permute-start.4) | collective-permute-done | bytes 524320 | tf_op jit(solution)/shard_map/ppermute | solution.py:177
  102.9 7.4 %collective-permute-done.5.second = f32[2,256,256]{2,1,0:T(8,128)S(1)} collective-permute-done((f32[2,256,256]{2,1,0:T(8,128)S(1)}, f32[2,256,256]{2,1,0:T(8,128)S(1)}, u32[]{:S(2)}, u32[]{:S(2)}) %collective-permute-start.5) | collective-permute-done | bytes 524320 | tf_op jit(solution)/shard_map/ppermute | solution.py:178
  110.3 2.2 %shard_map.56 = f32[4,256,256]{2,1,0:T(8,128)} custom-call(s32[1]{0:T(128)} %bitcast.1.even, f32[4,256,256]{2,1,0:T(8,128)S(1)} %bitcast.31, f32[2,256,256]{2,1,0:T(8,128)S(1)} %get-tuple-element.62.edge, f32[2,256,256]{2,1,0:T(8,128)S(1)} %collective-permute-done.4.first, f32[2,256,256]{2,1,0:T(8,128)S(1)} %collective-permute-done.5.second, ...), custom_call_target="tpu_custom_call" | custom-call | flops 3145728 | bytes 5242880 | tf_op jit(solution)/shard_map/pallas_call | solution.py:182
  (25 shorter events, 0.4 us)
Async XLA Ops:
  0.0 13.4 %copy-start.4 = (s32[16]{0:T(128)S(1)}, s32[16]{0:T(128)}, u32[]{:S(2)}) copy-start(s32[16]{0:T(128)} %constant.85.clone) | copy-start | bytes 196
  0.0 13.6 %copy-start.2 = (s32[32]{0:T(128)S(1)}, s32[32]{0:T(128)}, u32[]{:S(2)}) copy-start(s32[32]{0:T(128)} %constant.84.clone) | copy-start | bytes 388
  0.0 9.4 %copy-start.3 = (s32[32]{0:T(128)S(1)}, s32[32]{0:T(128)}, u32[]{:S(2)}) copy-start(s32[32]{0:T(128)} %param.11) | copy-start | bytes 388
  0.0 36.3 %all-to-all-start = ((f32[16,64,256]{2,1,0:T(8,128)}), f32[16,64,256]{2,1,0:T(8,128)S(1)}, u32[]{:S(2)}, u32[]{:S(2)}) async-start(f32[16,64,256]{2,1,0:T(8,128)} %bitcast.36), calls=%async_computation | async-start | bytes 2097152 | tf_op jit(solution)/shard_map/all_to_all | solution.py:31
  37.0 13.4 %collective-permute-start.1 = (f32[2,64,256]{2,1,0:T(8,128)S(1)}, f32[2,64,256]{2,1,0:T(8,128)S(1)}, u32[]{:S(2)}, u32[]{:S(2)}) collective-permute-start(f32[2,64,256]{2,1,0:T(8,128)S(1)} %gather_fusion.2), channel_id=1, source_target_pairs={{0,256},{16,272},{32,288},{48,304},{64,320},{80,336},{96,352},{112... | collective-permute-start | bytes 393224 | tf_op jit(solution)/shard_map/cond/branch_2_fun/ppermute | solution.py:71
  52.1 4.4 %copy-start = (f32[2,1,4,256,256]{4,3,2,1,0:T(8,128)S(1)}, f32[2,1,4,256,256]{4,3,2,1,0:T(8,128)}, u32[]{:S(2)}) copy-start(f32[2,1,4,256,256]{4,3,2,1,0:T(8,128)} %param.12) | copy-start | bytes 6291460
  52.1 31.2 %all-to-all-start.1 = ((f32[16,64,256]{2,1,0:T(8,128)}), f32[16,64,256]{2,1,0:T(8,128)S(1)}, u32[]{:S(2)}, u32[]{:S(2)}) async-start(f32[16,64,256]{2,1,0:T(8,128)} %get-tuple-element.164), calls=%async_computation.1 | async-start | bytes 2097152 | tf_op jit(solution)/shard_map/all_to_all | solution.py:31
  84.5 1.0 copy-start.1
  86.3 16.5 %collective-permute-start.4 = (f32[2,256,256]{2,1,0:T(8,128)S(1)}, f32[2,256,256]{2,1,0:T(8,128)S(1)}, u32[]{:S(2)}, u32[]{:S(2)}) collective-permute-start(f32[2,256,256]{2,1,0:T(8,128)S(1)} %get-tuple-element.63), channel_id=1, source_target_pairs={{0,1},{1,0},{2,3},{3,2},{4,5},{5,4},{6,7},{7,6},{8,9},{9,8},{10,11... | collective-permute-start | bytes 1572872 | tf_op jit(solution)/shard_map/ppermute | solution.py:177
  89.8 20.5 %collective-permute-start.5 = (f32[2,256,256]{2,1,0:T(8,128)S(1)}, f32[2,256,256]{2,1,0:T(8,128)S(1)}, u32[]{:S(2)}, u32[]{:S(2)}) collective-permute-start(f32[2,256,256]{2,1,0:T(8,128)S(1)} %get-tuple-element.64), channel_id=1, source_target_pairs={{0,15},{1,2},{2,1},{3,4},{4,3},{5,6},{6,5},{7,8},{8,7},{9,10},{10,... | collective-permute-start | bytes 1572872 | tf_op jit(solution)/shard_map/ppermute | solution.py:178

commit v2 on v1

--- a/solution.py
+++ b/solution.py
@@ -66,10 +66,15 @@
     swap = [(i, (i + HALF) % (2 * HALF)) for i in range(2 * HALF)]
 
     def crossing(width, spread, pick, send):
-        if width == 0:
-            return jnp.take(spread, pick, axis=0, mode="clip")
-        far = lax.ppermute(jnp.take(spread, send[:width], axis=0, mode="clip"), "rep", swap)
-        return jnp.take(jnp.concatenate([spread, far]), pick, axis=0, mode="clip")
+        if width == HALF:
+            far = lax.ppermute(jnp.take(spread, send, axis=0, mode="clip"), "rep", swap)
+            return jnp.take(jnp.concatenate([spread, far]), pick, axis=0, mode="clip")
+        if width:
+            far = lax.ppermute(jnp.take(spread, send[:width], axis=0, mode="clip"), "rep", swap)
+        parts = jnp.take(spread, pick, axis=0, mode="clip")
+        for i in range(width):
+            parts = jnp.where((pick == HALF + i)[:, None, None], far[i : i + 1], parts)
+        return parts
 
     widths = (0, 1, 2, 4, HALF)
     case = sum((count > w).astype(jnp.int32) for w in widths[:-1])
@@ -95,10 +100,13 @@
         body(start, pl.ds(start, STRIP))
 
 
-def edge_kernel(even, field, noise, edge, inner, outer):
+def edge_kernel(even, field, noise, edge, middle, inner, outer):
     def body(start, here):
         edge[0, here, :] = step(field, 0, start, field[1, here, :], KICK * noise[0, 0, here, :])
         edge[1, here, :] = step(field, 3, start, field[2, here, :], KICK * noise[0, 3, here, :])
+        for plane in (1, 2):
+            along_z = field[plane + 1, here, :] + field[plane - 1, here, :]
+            middle[plane - 1, here, :] = step(field, plane, start, along_z, KICK * noise[0, plane, here, :])
 
     strips(body)
 
@@ -146,6 +154,15 @@
     strips(end)
 
 
+def side_swap(turn, size):
+    pairs = []
+    for rep in range(2 * HALF):
+        for slab in range(size):
+            above = (slab + rep + turn) % 2 == 0
+            pairs.append((rep * size + slab, rep * size + (slab + (1 if above else -1)) % size))
+    return pairs
+
+
 def swept(center, along_z, kicks):
     total = along_z + jnp.roll(center, -1, 1) + jnp.roll(center, 1, 1)
     total = total + jnp.roll(center, -1, 2) + jnp.roll(center, 1, 2)
@@ -162,21 +179,19 @@
     spread = exchange(phi_field.reshape(HALF, -1, width), order)
     route = routes(copy_counts, order)
     field = exchange(chosen_parts(spread, *route), order).reshape(planes, height, width)
-    even = (lax.axis_index("slab") % 2 == 0).astype(jnp.int32).reshape(1)
+    even = ((lax.axis_index("slab") + lax.axis_index("rep")) % 2 == 0).astype(jnp.int32).reshape(1)
     pair = jax.ShapeDtypeStruct((2, height, width), jnp.float32)
     plane = 4 * height * width
-    edge, inner, outer = pl.pallas_call(
+    edge, middle, inner, outer = pl.pallas_call(
         edge_kernel,
-        out_shape=[pair] * 3,
+        out_shape=[pair] * 4,
         in_specs=[SMEM] + [VMEM] * 2,
-        out_specs=[VMEM] * 3,
+        out_specs=[VMEM] * 4,
         compiler_params=PARAMS,
         cost_estimate=cost(2 * 16 * plane // 4, 12 * plane),
     )(even, field, noise)
-    inner, outer, field = lax.optimization_barrier((inner, outer, field))
-    first = lax.ppermute(inner, "slab", [(i, i ^ 1) for i in range(size)])
-    second = lax.ppermute(outer, "slab", [(i, (i - 1 + 2 * (i % 2)) % size) for i in range(size)])
-    middle = swept(field[1:3], field[2:4] + field[0:2], noise[0, 1:3])
+    first = lax.ppermute(inner, ("rep", "slab"), side_swap(0, size))
+    second = lax.ppermute(outer, ("rep", "slab"), side_swap(1, size))
     later = swept(middle, middle[::-1], noise[1, 1:3])
     last = KICK * jnp.concatenate([noise[1, :1], noise[1, 3:]])
     out = pl.pallas_call(

time: 113 us -> 105 us (0.929)
  waiting for transfers between devices: 66.6 us -> 60.7 us
  local copies, waits for them, and re-layouts: 4.46 us -> 1.13 us
    ppermute x2, waiting for transfers between devices: 13.7 us -> 10.1 us  [the longest x1 9.25 us: shards(): second = lax.ppermute(outer, ('rep', 'slab'), side_swap(1, size))]
    ppermute x1, waiting for transfers between devices: 4.42 us -> 2.37 us  [crossing(): lax.ppermute(jnp.take(spread, send[:width], axis=0, mode='clip'), 'rep',...]
  transfers between devices with their start and end apart: 5 -> 5, of which waited for: 5 -> 5; matrix products, arithmetic and copies ran while one was open for 3% -> 4% of each run, Pallas kernels for 0% -> 0%
where the time goes in v2:
time: 105 us
  waiting for transfers between devices  60.7 us (58%)
  starting transfers between devices  32.7 us (31%)
  other arithmetic  4.06 us (4%)
  Pallas kernels  3.43 us (3%)
  between operations  2.76 us (3%)
  local copies, waits for them, and re-layouts  1.13 us (1%)
    all_to_all x2, waiting for transfers between devices, exchange(): lax.all_to_all(parts, 'rep', split_axis=0, concat_axis=0, tiled=True, axi...  48.2 us
    all_to_all x2, starting transfers between devices, exchange(): lax.all_to_all(parts, 'rep', split_axis=0, concat_axis=0, tiled=True, axi...  14.3 us
    ppermute x1, waiting for transfers between devices, shards(): second = lax.ppermute(outer, ('rep', 'slab'), side_swap(1, size))  9.25 us
    ppermute x1, starting transfers between devices, crossing(): lax.ppermute(jnp.take(spread, send[:width], axis=0, mode='clip'), 'rep',...  8.94 us
    ppermute x1, starting transfers between devices, shards(): second = lax.ppermute(outer, ('rep', 'slab'), side_swap(1, size))  6.12 us
    ppermute x1, starting transfers between devices, shards(): first = lax.ppermute(inner, ('rep', 'slab'), side_swap(0, size))  3.4 us
    ppermute x1, waiting for transfers between devices, crossing(): lax.ppermute(jnp.take(spread, send[:width], axis=0, mode='clip'), 'rep',...  2.37 us
    pallas_call x1, Pallas kernels, shards(): pl.pallas_call(late_kernel, out_shape=jax.ShapeDtypeStruct((planes, heigh...  2.13 us
  transfers between devices with their start and end apart: 5, of which 5 were waited for; matrix products, arithmetic and copies ran while one was open for 4% of the time, Pallas kernels for 0%

profile of v2, /device:TPU:8, one launch (start us, length us, event | category | flops | bytes accessed | tf_op | source)
XLA Modules:
  0.0 104.8 jit_solution(7450494935263914263)
XLA Ops:
  0.0 9.4 %all-to-all-start = ((f32[16,64,256]{2,1,0:T(8,128)}), f32[16,64,256]{2,1,0:T(8,128)S(1)}, u32[]{:S(2)}, u32[]{:S(2)}) async-start(f32[16,64,256]{2,1,0:T(8,128)} %bitcast.36), calls=%async_computation | async-start | bytes 2097152 | tf_op jit(solution)/shard_map/all_to_all | solution.py:31
  9.4 0.0 copy-done.2
  9.5 0.1 select_reduce_fusion
  9.6 0.1 select_reduce_fusion.1
  9.7 0.2 convert_reduce_fusion.1
  9.9 0.1 fusion.11
  10.0 0.6 convert_reduce_fusion.2
  13.3 0.1 convert_reduce_fusion
  13.4 0.0 copy-done.4
  13.4 0.2 select_reduce_fusion.4
  13.6 0.0 copy-done.3
  13.6 0.2 select_reduce_fusion.2
  13.8 22.5 %all-to-all-done = f32[16,64,256]{2,1,0:T(8,128)S(1)} async-done(((f32[16,64,256]{2,1,0:T(8,128)}), f32[16,64,256]{2,1,0:T(8,128)S(1)}, u32[]{:S(2)}, u32[]{:S(2)}) %all-to-all-start) | async-done | bytes 1048608 | tf_op jit(solution)/shard_map/all_to_all | solution.py:31
  36.3 13.1 %conditional.1 = (f32[16,64,256]{2,1,0:T(8,128)}) conditional(s32[]{:T(128)} %clamp.3, (s32[16]{0:T(128)S(1)}, f32[16,64,256]{2,1,0:T(8,128)S(1)}) %tuple.20, (s32[16]{0:T(128)S(1)}, s32[16]{0:T(128)S(1)}, f32[16,64,256]{2,1,0:T(8,128)S(1)}) %tuple.21, (s32[16]{0:T(128)S(1)}, s32[16]{0:T(128)S(1)}, ...), branch_computations={%region_9.10_spmd, %region_10.11_spmd, %region_11.12_spmd, %region... | conditional | flops 1050688 | bytes 12591408 | solution.py:81
  36.3 8.9 %collective-permute-start.3 = (f32[1,64,256]{2,1,0:T(8,128)S(1)}, f32[1,64,256]{2,1,0:T(8,128)S(1)}, u32[]{:S(2)}, u32[]{:S(2)}) collective-permute-start(f32[1,64,256]{2,1,0:T(8,128)S(1)} %constant_dynamic-slice_fusion), channel_id=1, source_target_pairs={{0,256},{16,272},{32,288},{48,304},{64,320},{80,336},{96,352},{112... | collective-permute-start | bytes 196616 | tf_op jit(solution)/shard_map/cond/branch_1_fun/ppermute | solution.py:73
  45.3 0.6 gather_fusion.7
  45.9 2.4 %collective-permute-done.3 = f32[1,64,256]{2,1,0:T(8,128)S(1)} collective-permute-done((f32[1,64,256]{2,1,0:T(8,128)S(1)}, f32[1,64,256]{2,1,0:T(8,128)S(1)}, u32[]{:S(2)}, u32[]{:S(2)}) %collective-permute-start.3) | collective-permute-done | bytes 65568 | tf_op jit(solution)/shard_map/cond/branch_1_fun/ppermute | solution.py:73
  48.3 1.1 %broadcast_select_fusion = f32[16,64,256]{2,1,0:T(8,128)} fusion(f32[16,64,256]{2,1,0:T(8,128)S(1)} %gather_fusion.7, f32[64,256]{1,0:T(8,128)S(1)} %bitcast.37, pred[16]{0:T(512)(128)(4,1)S(1)} %broadcast_compare_fusion.6), kind=kLoop, calls=%fused_computation.30 | loop fusion | flops 262144 | bytes 2162704 | tf_op jit(solution)/shard_map/cond/branch_1_fun/jit(_where)/select_n | solution.py:76
  49.4 4.8 %all-to-all-start.1 = ((f32[16,64,256]{2,1,0:T(8,128)}), f32[16,64,256]{2,1,0:T(8,128)S(1)}, u32[]{:S(2)}, u32[]{:S(2)}) async-start(f32[16,64,256]{2,1,0:T(8,128)} %get-tuple-element.100), calls=%async_computation.1 | async-start | bytes 2097152 | tf_op jit(solution)/shard_map/all_to_all | solution.py:31
  54.2 0.0 copy-done
  54.3 0.8 maximum_multiply_fusion.last
  55.1 25.7 %all-to-all-done.1 = f32[16,64,256]{2,1,0:T(8,128)S(1)} async-done(((f32[16,64,256]{2,1,0:T(8,128)}), f32[16,64,256]{2,1,0:T(8,128)S(1)}, u32[]{:S(2)}, u32[]{:S(2)}) %all-to-all-start.1) | async-done | bytes 1048608 | tf_op jit(solution)/shard_map/all_to_all | solution.py:31
  80.8 1.3 %shard_map.55 = (f32[2,256,256]{2,1,0:T(8,128)S(1)}, f32[2,256,256]{2,1,0:T(8,128)S(1)}, f32[2,256,256]{2,1,0:T(8,128)S(1)}, f32[2,256,256]{2,1,0:T(8,128)S(1)}) custom-call(s32[1]{0:T(128)} %bitcast.8.even, f32[4,256,256]{2,1,0:T(8,128)S(1)} %bitcast.31, f32[2,4,256,256]{3,2,1,0:T(8,128)S(1)} %bitcast.34), custom_call_target="tpu_custom_call" | custom-call | flops 2097152 | bytes 3145728 | tf_op jit(solution)/shard_map/pallas_call | solution.py:185
  82.1 0.1 fusion.18
  82.2 0.1 fusion.15
  82.4 3.4 %collective-permute-start.4 = (f32[2,256,256]{2,1,0:T(8,128)S(1)}, f32[2,256,256]{2,1,0:T(8,128)S(1)}, u32[]{:S(2)}, u32[]{:S(2)}) collective-permute-start(f32[2,256,256]{2,1,0:T(8,128)S(1)} %get-tuple-element.58), channel_id=1, source_target_pairs={{0,1},{1,0},{2,3},{3,2},{4,5},{5,4},{6,7},{7,6},{8,9},{9,8},{10,11... | collective-permute-start | bytes 1572872 | tf_op jit(solution)/shard_map/ppermute | solution.py:193
  85.8 6.1 %collective-permute-start.5 = (f32[2,256,256]{2,1,0:T(8,128)S(1)}, f32[2,256,256]{2,1,0:T(8,128)S(1)}, u32[]{:S(2)}, u32[]{:S(2)}) collective-permute-start(f32[2,256,256]{2,1,0:T(8,128)S(1)} %get-tuple-element.59), channel_id=1, source_target_pairs={{0,15},{1,2},{2,1},{3,4},{4,3},{5,6},{6,5},{7,8},{8,7},{9,10},{10,... | collective-permute-start | bytes 1572872 | tf_op jit(solution)/shard_map/ppermute | solution.py:194
  91.9 0.2 fusion.16
  92.1 0.4 fusion.3.later
  92.5 0.9 collective-permute-done.4.first
  93.4 9.2 %collective-permute-done.5.second = f32[2,256,256]{2,1,0:T(8,128)S(1)} collective-permute-done((f32[2,256,256]{2,1,0:T(8,128)S(1)}, f32[2,256,256]{2,1,0:T(8,128)S(1)}, u32[]{:S(2)}, u32[]{:S(2)}) %collective-permute-start.5) | collective-permute-done | bytes 524320 | tf_op jit(solution)/shard_map/ppermute | solution.py:194
  102.7 2.1 %shard_map.56 = f32[4,256,256]{2,1,0:T(8,128)} custom-call(s32[1]{0:T(128)} %bitcast.8.even, f32[4,256,256]{2,1,0:T(8,128)S(1)} %bitcast.32, f32[2,256,256]{2,1,0:T(8,128)S(1)} %get-tuple-element.57.edge, f32[2,256,256]{2,1,0:T(8,128)S(1)} %collective-permute-done.4.first, f32[2,256,256]{2,1,0:T(8,128)S(1)} %collective-permute-done.5.second, ...), custom_call_target="tpu_custom_call" | custom-call | flops 3145728 | bytes 5242880 | tf_op jit(solution)/shard_map/pallas_call | solution.py:197
  (18 shorter events, 0.2 us)
Async XLA Ops:
  0.0 13.4 %copy-start.4 = (s32[16]{0:T(128)S(1)}, s32[16]{0:T(128)}, u32[]{:S(2)}) copy-start(s32[16]{0:T(128)} %constant.99.clone) | copy-start | bytes 196
  0.0 13.6 %copy-start.3 = (s32[32]{0:T(128)S(1)}, s32[32]{0:T(128)}, u32[]{:S(2)}) copy-start(s32[32]{0:T(128)} %constant.98.clone) | copy-start | bytes 388
  0.0 9.4 %copy-start.2 = (s32[32]{0:T(128)S(1)}, s32[32]{0:T(128)}, u32[]{:S(2)}) copy-start(s32[32]{0:T(128)} %param.11) | copy-start | bytes 388
  0.0 36.3 %all-to-all-start = ((f32[16,64,256]{2,1,0:T(8,128)}), f32[16,64,256]{2,1,0:T(8,128)S(1)}, u32[]{:S(2)}, u32[]{:S(2)}) async-start(f32[16,64,256]{2,1,0:T(8,128)} %bitcast.36), calls=%async_computation | async-start | bytes 2097152 | tf_op jit(solution)/shard_map/all_to_all | solution.py:31
  36.3 12.0 %collective-permute-start.3 = (f32[1,64,256]{2,1,0:T(8,128)S(1)}, f32[1,64,256]{2,1,0:T(8,128)S(1)}, u32[]{:S(2)}, u32[]{:S(2)}) collective-permute-start(f32[1,64,256]{2,1,0:T(8,128)S(1)} %constant_dynamic-slice_fusion), channel_id=1, source_target_pairs={{0,256},{16,272},{32,288},{48,304},{64,320},{80,336},{96,352},{112... | collective-permute-start | bytes 196616 | tf_op jit(solution)/shard_map/cond/branch_1_fun/ppermute | solution.py:73
  49.4 4.9 %copy-start = (f32[2,1,4,256,256]{4,3,2,1,0:T(8,128)S(1)}, f32[2,1,4,256,256]{4,3,2,1,0:T(8,128)}, u32[]{:S(2)}) copy-start(f32[2,1,4,256,256]{4,3,2,1,0:T(8,128)} %param.12) | copy-start | bytes 6291460
  49.4 31.4 %all-to-all-start.1 = ((f32[16,64,256]{2,1,0:T(8,128)}), f32[16,64,256]{2,1,0:T(8,128)S(1)}, u32[]{:S(2)}, u32[]{:S(2)}) async-start(f32[16,64,256]{2,1,0:T(8,128)} %get-tuple-element.100), calls=%async_computation.1 | async-start | bytes 2097152 | tf_op jit(solution)/shard_map/all_to_all | solution.py:31
  82.4 11.1 %collective-permute-start.4 = (f32[2,256,256]{2,1,0:T(8,128)S(1)}, f32[2,256,256]{2,1,0:T(8,128)S(1)}, u32[]{:S(2)}, u32[]{:S(2)}) collective-permute-start(f32[2,256,256]{2,1,0:T(8,128)S(1)} %get-tuple-element.58), channel_id=1, source_target_pairs={{0,1},{1,0},{2,3},{3,2},{4,5},{5,4},{6,7},{7,6},{8,9},{9,8},{10,11... | collective-permute-start | bytes 1572872 | tf_op jit(solution)/shard_map/ppermute | solution.py:193
  85.8 16.9 %collective-permute-start.5 = (f32[2,256,256]{2,1,0:T(8,128)S(1)}, f32[2,256,256]{2,1,0:T(8,128)S(1)}, u32[]{:S(2)}, u32[]{:S(2)}) collective-permute-start(f32[2,256,256]{2,1,0:T(8,128)S(1)} %get-tuple-element.59), channel_id=1, source_target_pairs={{0,15},{1,2},{2,1},{3,4},{4,3},{5,6},{6,5},{7,8},{8,7},{9,10},{10,... | collective-permute-start | bytes 1572872 | tf_op jit(solution)/shard_map/ppermute | solution.py:194
  92.1 10.6 %copy-start.1 = (f32[2,256,256]{2,1,0:T(8,128)S(1)}, f32[2,256,256]{2,1,0:T(8,128)}, u32[]{:S(2)}) copy-start(f32[2,256,256]{2,1,0:T(8,128)} %maximum_multiply_fusion.last) | copy-start | bytes 1572868

commit v3 on v2

--- a/solution.py
+++ b/solution.py
@@ -59,26 +59,28 @@
     where_from = jnp.where(ids // HALF == half, place, HALF + rank)
     source = jnp.sum(jnp.where(target[:, None] == ids[None, :], source_map[None, :], 0), axis=1)
     pick = jnp.sum(jnp.where(source[:, None] == ids[None, :], where_from[None, :], 0), axis=1)
-    return pick, send, count
-
-
-def chosen_parts(spread, pick, send, count):
-    swap = [(i, (i + HALF) % (2 * HALF)) for i in range(2 * HALF)]
-
-    def crossing(width, spread, pick, send):
+    return pick, send, count, jnp.any(wanted[:HALF])
+
+
+def chosen_parts(spread, pick, send, count, upward):
+    def kept(spread, pick, send):
+        return jnp.take(spread, pick, axis=0, mode="clip")
+
+    def crossing(width, source, spread, pick, send):
+        pairs = [(source * HALF + i, (1 - source) * HALF + i) for i in range(HALF)]
+        far = lax.ppermute(jnp.take(spread, send[:width], axis=0, mode="clip"), "rep", pairs)
         if width == HALF:
-            far = lax.ppermute(jnp.take(spread, send, axis=0, mode="clip"), "rep", swap)
             return jnp.take(jnp.concatenate([spread, far]), pick, axis=0, mode="clip")
-        if width:
-            far = lax.ppermute(jnp.take(spread, send[:width], axis=0, mode="clip"), "rep", swap)
-        parts = jnp.take(spread, pick, axis=0, mode="clip")
+        parts = kept(spread, pick, send)
         for i in range(width):
             parts = jnp.where((pick == HALF + i)[:, None, None], far[i : i + 1], parts)
         return parts
 
-    widths = (0, 1, 2, 4, HALF)
+    widths = (1, 2, 3, 4, 6, HALF)
     case = sum((count > w).astype(jnp.int32) for w in widths[:-1])
-    return lax.switch(case, [functools.partial(crossing, w) for w in widths], spread, pick, send)
+    case = jnp.where(count == 0, 0, 1 + case + jnp.where(upward, 0, len(widths)))
+    branches = [kept] + [functools.partial(crossing, w, source) for source in range(2) for w in widths]
+    return lax.switch(case, branches, spread, pick, send)
 
 
 def step(ref, plane, start, along_z, kicks):

time: 105 us -> 112 us (1.067)
  the two profiles are of different devices: /device:TPU:8 before, /device:TPU:72 now
where the time goes in v3:
time: 112 us; the launch traced here: 111 us
  waiting for transfers between devices  78 us (70%)
  starting transfers between devices  18.5 us (17%)
  other arithmetic  4.92 us (4%)
  between operations  4.71 us (4%)
  Pallas kernels  3.43 us (3%)
  local copies, waits for them, and re-layouts  1.67 us (1%)
    all_to_all x2, waiting for transfers between devices, exchange(): lax.all_to_all(parts, 'rep', split_axis=0, concat_axis=0, tiled=True, axi...  45.3 us
    ppermute x1, waiting for transfers between devices, crossing(): lax.ppermute(jnp.take(spread, send[:width], axis=0, mode='clip'), 'rep',...  20.2 us
    all_to_all x2, starting transfers between devices, exchange(): lax.all_to_all(parts, 'rep', split_axis=0, concat_axis=0, tiled=True, axi...  11.9 us
    ppermute x1, waiting for transfers between devices, shards(): first = lax.ppermute(inner, ('rep', 'slab'), side_swap(0, size))  8.02 us
    ppermute x1, waiting for transfers between devices, shards(): second = lax.ppermute(outer, ('rep', 'slab'), side_swap(1, size))  4.51 us
    ppermute x1, starting transfers between devices, shards(): first = lax.ppermute(inner, ('rep', 'slab'), side_swap(0, size))  3.4 us
  transfers between devices with their start and end apart: 5, of which 5 were waited for; matrix products, arithmetic and copies ran while one was open for 4% of the time, Pallas kernels for 0%

profile of v3, /device:TPU:72, one launch (start us, length us, event | category | flops | bytes accessed | tf_op | source)
XLA Modules:
  0.0 111.3 jit_solution(12924084644572011652)
XLA Ops:
  0.0 7.7 %all-to-all-start = ((f32[16,64,256]{2,1,0:T(8,128)}), f32[16,64,256]{2,1,0:T(8,128)S(1)}, u32[]{:S(2)}, u32[]{:S(2)}) async-start(f32[16,64,256]{2,1,0:T(8,128)} %bitcast.93), calls=%async_computation | async-start | bytes 2097152 | tf_op jit(solution)/shard_map/all_to_all | solution.py:31
  7.7 0.0 copy-done.2
  7.7 0.1 select_reduce_fusion
  7.9 0.1 select_reduce_fusion.1
  8.0 0.2 convert_reduce_fusion.1
  8.2 0.1 fusion.11
  8.3 0.6 convert_reduce_fusion.2
  12.8 0.6 slice_reduce_fusion
  14.1 0.1 convert_reduce_fusion
  14.2 0.0 copy-done.4
  14.3 0.2 select_reduce_fusion.4
  14.5 0.2 select_reduce_fusion.2
  14.7 19.6 %all-to-all-done = f32[16,64,256]{2,1,0:T(8,128)S(1)} async-done(((f32[16,64,256]{2,1,0:T(8,128)}), f32[16,64,256]{2,1,0:T(8,128)S(1)}, u32[]{:S(2)}, u32[]{:S(2)}) %all-to-all-start) | async-done | bytes 1048608 | tf_op jit(solution)/shard_map/all_to_all | solution.py:31
  34.3 24.1 %conditional.1 = (f32[16,64,256]{2,1,0:T(8,128)}) conditional(s32[]{:T(128)} %clamp.3, (s32[16]{0:T(128)S(1)}, f32[16,64,256]{2,1,0:T(8,128)S(1)}) %tuple.44, (s32[16]{0:T(128)S(1)}, s32[16]{0:T(128)S(1)}, f32[16,64,256]{2,1,0:T(8,128)S(1)}) %tuple.45, (s32[16]{0:T(128)S(1)}, s32[16]{0:T(128)S(1)}, ...), branch_computations={%region_10.11_spmd, %region_11.12_spmd, %region_12.13_spmd, %regio... | conditional | flops 1575008 | bytes 12591408 | solution.py:83
  34.3 0.6 gather_fusion.15
  34.9 1.3 %collective-permute-start.7 = (f32[4,64,256]{2,1,0:T(8,128)S(1)}, f32[4,64,256]{2,1,0:T(8,128)S(1)}, u32[]{:S(2)}, u32[]{:S(2)}) collective-permute-start(f32[4,64,256]{2,1,0:T(8,128)S(1)} %gather_fusion.15), channel_id=1, source_target_pairs={{256,0},{272,16},{288,32},{304,48},{320,64},{336,80},{352,96},{368... | collective-permute-start | bytes 786440 | tf_op jit(solution)/shard_map/cond/branch_10_fun/ppermute | solution.py:71
  36.2 0.6 gather_fusion.16
  36.8 20.2 %collective-permute-done.7 = f32[4,64,256]{2,1,0:T(8,128)S(1)} collective-permute-done((f32[4,64,256]{2,1,0:T(8,128)S(1)}, f32[4,64,256]{2,1,0:T(8,128)S(1)}, u32[]{:S(2)}, u32[]{:S(2)}) %collective-permute-start.7) | collective-permute-done | bytes 262176 | tf_op jit(solution)/shard_map/cond/branch_10_fun/ppermute | solution.py:71
  57.0 1.3 %select_select_fusion.6 = f32[16,64,256]{2,1,0:T(8,128)} fusion(f32[16,64,256]{2,1,0:T(8,128)S(1)} %gather_fusion.16, f32[64,256]{1,0:T(8,128)S(1)} %get-tuple-element.206, f32[64,256]{1,0:T(8,128)S(1)} %get-tuple-element.207, f32[64,256]{1,0:T(8,128)S(1)} %get-tuple-element.208, f32[64,256]{1,0:T(8,128)S(1)} %get-tuple-element.205, ...), kind=kLoop, calls=%fused_computation.85 | loop fusion | flops 1048576 | bytes 2359360 | tf_op jit(solution)/shard_map/cond/branch_10_fun/jit(_where)/select_n | solution.py:76
  58.4 4.2 %all-to-all-start.1 = ((f32[16,64,256]{2,1,0:T(8,128)}), f32[16,64,256]{2,1,0:T(8,128)S(1)}, u32[]{:S(2)}, u32[]{:S(2)}) async-start(f32[16,64,256]{2,1,0:T(8,128)} %get-tuple-element.239), calls=%async_computation.1 | async-start | bytes 2097152 | tf_op jit(solution)/shard_map/all_to_all | solution.py:31
  62.6 0.9 maximum_multiply_fusion.last
  63.4 25.7 %all-to-all-done.1 = f32[16,64,256]{2,1,0:T(8,128)S(1)} async-done(((f32[16,64,256]{2,1,0:T(8,128)}), f32[16,64,256]{2,1,0:T(8,128)S(1)}, u32[]{:S(2)}, u32[]{:S(2)}) %all-to-all-start.1) | async-done | bytes 1048608 | tf_op jit(solution)/shard_map/all_to_all | solution.py:31
  89.1 1.3 %shard_map.55 = (f32[2,256,256]{2,1,0:T(8,128)S(1)}, f32[2,256,256]{2,1,0:T(8,128)S(1)}, f32[2,256,256]{2,1,0:T(8,128)S(1)}, f32[2,256,256]{2,1,0:T(8,128)S(1)}) custom-call(s32[1]{0:T(128)} %bitcast.34.even, f32[4,256,256]{2,1,0:T(8,128)S(1)} %bitcast.88, f32[2,4,256,256]{3,2,1,0:T(8,128)S(1)} %bitcast.91), custom_call_target="tpu_custom_call" | custom-call | flops 2097152 | bytes 3145728 | tf_op jit(solution)/shard_map/pallas_call | solution.py:187
  90.4 0.1 fusion.18
  90.5 0.1 fusion.15
  90.6 3.4 %collective-permute-start.12 = (f32[2,256,256]{2,1,0:T(8,128)S(1)}, f32[2,256,256]{2,1,0:T(8,128)S(1)}, u32[]{:S(2)}, u32[]{:S(2)}) collective-permute-start(f32[2,256,256]{2,1,0:T(8,128)S(1)} %get-tuple-element.138), channel_id=1, source_target_pairs={{0,1},{1,0},{2,3},{3,2},{4,5},{5,4},{6,7},{7,6},{8,9},{9,8},{10,11... | collective-permute-start | bytes 1572872 | tf_op jit(solution)/shard_map/ppermute | solution.py:195
  94.0 1.9 %collective-permute-start.13 = (f32[2,256,256]{2,1,0:T(8,128)S(1)}, f32[2,256,256]{2,1,0:T(8,128)S(1)}, u32[]{:S(2)}, u32[]{:S(2)}) collective-permute-start(f32[2,256,256]{2,1,0:T(8,128)S(1)} %get-tuple-element.139), channel_id=1, source_target_pairs={{0,15},{1,2},{2,1},{3,4},{4,3},{5,6},{6,5},{7,8},{8,7},{9,10},{10,... | collective-permute-start | bytes 1572872 | tf_op jit(solution)/shard_map/ppermute | solution.py:196
  96.0 0.2 fusion.16
  96.2 0.4 fusion.3.later
  96.6 8.0 %collective-permute-done.12.first = f32[2,256,256]{2,1,0:T(8,128)S(1)} collective-permute-done((f32[2,256,256]{2,1,0:T(8,128)S(1)}, f32[2,256,256]{2,1,0:T(8,128)S(1)}, u32[]{:S(2)}, u32[]{:S(2)}) %collective-permute-start.12) | collective-permute-done | bytes 524320 | tf_op jit(solution)/shard_map/ppermute | solution.py:195
  104.6 4.5 %collective-permute-done.13.second = f32[2,256,256]{2,1,0:T(8,128)S(1)} collective-permute-done((f32[2,256,256]{2,1,0:T(8,128)S(1)}, f32[2,256,256]{2,1,0:T(8,128)S(1)}, u32[]{:S(2)}, u32[]{:S(2)}) %collective-permute-start.13) | collective-permute-done | bytes 524320 | tf_op jit(solution)/shard_map/ppermute | solution.py:196
  109.1 2.1 %shard_map.56 = f32[4,256,256]{2,1,0:T(8,128)} custom-call(s32[1]{0:T(128)} %bitcast.34.even, f32[4,256,256]{2,1,0:T(8,128)S(1)} %bitcast.89, f32[2,256,256]{2,1,0:T(8,128)S(1)} %get-tuple-element.137.edge, f32[2,256,256]{2,1,0:T(8,128)S(1)} %collective-permute-done.12.first, f32[2,256,256]{2,1,0:T(8,128)S(1)} %collective-permute-done.13.second, ...), custom_call_target="tpu_custom_call" | custom-call | flops 3145728 | bytes 5242880 | tf_op jit(solution)/shard_map/pallas_call | solution.py:199
  (21 shorter events, 0.1 us)
Async XLA Ops:
  0.0 14.2 %copy-start.4 = (s32[16]{0:T(128)S(1)}, s32[16]{0:T(128)}, u32[]{:S(2)}) copy-start(s32[16]{0:T(128)} %constant.155.clone) | copy-start | bytes 196
  0.0 14.4 %copy-start.3 = (s32[32]{0:T(128)S(1)}, s32[32]{0:T(128)}, u32[]{:S(2)}) copy-start(s32[32]{0:T(128)} %constant.154.clone) | copy-start | bytes 388
  0.0 7.7 %copy-start.2 = (s32[32]{0:T(128)S(1)}, s32[32]{0:T(128)}, u32[]{:S(2)}) copy-start(s32[32]{0:T(128)} %param.19) | copy-start | bytes 388
  0.0 34.3 %all-to-all-start = ((f32[16,64,256]{2,1,0:T(8,128)}), f32[16,64,256]{2,1,0:T(8,128)S(1)}, u32[]{:S(2)}, u32[]{:S(2)}) async-start(f32[16,64,256]{2,1,0:T(8,128)} %bitcast.93), calls=%async_computation | async-start | bytes 2097152 | tf_op jit(solution)/shard_map/all_to_all | solution.py:31
  34.9 22.2 %collective-permute-start.7 = (f32[4,64,256]{2,1,0:T(8,128)S(1)}, f32[4,64,256]{2,1,0:T(8,128)S(1)}, u32[]{:S(2)}, u32[]{:S(2)}) collective-permute-start(f32[4,64,256]{2,1,0:T(8,128)S(1)} %gather_fusion.15), channel_id=1, source_target_pairs={{256,0},{272,16},{288,32},{304,48},{320,64},{336,80},{352,96},{368... | collective-permute-start | bytes 786440 | tf_op jit(solution)/shard_map/cond/branch_10_fun/ppermute | solution.py:71
  58.4 4.2 %copy-start = (f32[2,1,4,256,256]{4,3,2,1,0:T(8,128)S(1)}, f32[2,1,4,256,256]{4,3,2,1,0:T(8,128)}, u32[]{:S(2)}) copy-start(f32[2,1,4,256,256]{4,3,2,1,0:T(8,128)} %param.20) | copy-start | bytes 6291460
  58.4 30.7 %all-to-all-start.1 = ((f32[16,64,256]{2,1,0:T(8,128)}), f32[16,64,256]{2,1,0:T(8,128)S(1)}, u32[]{:S(2)}, u32[]{:S(2)}) async-start(f32[16,64,256]{2,1,0:T(8,128)} %get-tuple-element.239), calls=%async_computation.1 | async-start | bytes 2097152 | tf_op jit(solution)/shard_map/all_to_all | solution.py:31
  90.6 14.0 %collective-permute-start.12 = (f32[2,256,256]{2,1,0:T(8,128)S(1)}, f32[2,256,256]{2,1,0:T(8,128)S(1)}, u32[]{:S(2)}, u32[]{:S(2)}) collective-permute-start(f32[2,256,256]{2,1,0:T(8,128)S(1)} %get-tuple-element.138), channel_id=1, source_target_pairs={{0,1},{1,0},{2,3},{3,2},{4,5},{5,4},{6,7},{7,6},{8,9},{9,8},{10,11... | collective-permute-start | bytes 1572872 | tf_op jit(solution)/shard_map/ppermute | solution.py:195
  94.0 15.1 %collective-permute-start.13 = (f32[2,256,256]{2,1,0:T(8,128)S(1)}, f32[2,256,256]{2,1,0:T(8,128)S(1)}, u32[]{:S(2)}, u32[]{:S(2)}) collective-permute-start(f32[2,256,256]{2,1,0:T(8,128)S(1)} %get-tuple-element.139), channel_id=1, source_target_pairs={{0,15},{1,2},{2,1},{3,4},{4,3},{5,6},{6,5},{7,8},{8,7},{9,10},{10,... | collective-permute-start | bytes 1572872 | tf_op jit(solution)/shard_map/ppermute | solution.py:196
  96.2 13.0 %copy-start.1 = (f32[2,256,256]{2,1,0:T(8,128)S(1)}, f32[2,256,256]{2,1,0:T(8,128)}, u32[]{:S(2)}) copy-start(f32[2,256,256]{2,1,0:T(8,128)} %maximum_multiply_fusion.last) | copy-start | bytes 1572868

commit v4 on v3

--- a/solution.py
+++ b/solution.py
@@ -12,9 +12,10 @@
 COUPLING = 0.5
 KICK = (2.0 * STEP_SIZE) ** 0.5
 HALF = 16
-STRIP = 32
+STRIP = 64
 VMEM = pl.BlockSpec(memory_space=pltpu.VMEM)
 SMEM = pl.BlockSpec(memory_space=pltpu.SMEM)
+HBM = pl.BlockSpec(memory_space=pl.ANY)
 PARAMS = pltpu.CompilerParams(vmem_limit_bytes=10 * 1024 * 1024)
 
 
@@ -102,58 +103,96 @@
         body(start, pl.ds(start, STRIP))
 
 
-def edge_kernel(even, field, noise, edge, middle, inner, outer):
-    def body(start, here):
-        edge[0, here, :] = step(field, 0, start, field[1, here, :], KICK * noise[0, 0, here, :])
-        edge[1, here, :] = step(field, 3, start, field[2, here, :], KICK * noise[0, 3, here, :])
+def edge_kernel(even, field, noise, edge, inner, outer):
+    def fill(below, above):
+        def body(start, here):
+            low = step(field, 0, start, field[1, here, :], KICK * noise[0, 0, here, :])
+            high = step(field, 3, start, field[2, here, :], KICK * noise[0, 3, here, :])
+            edge[0, here, :] = low
+            edge[1, here, :] = high
+            below[0, here, :] = field[0, here, :]
+            below[1, here, :] = low
+            above[0, here, :] = field[3, here, :]
+            above[1, here, :] = high
+
+        strips(body)
+
+    @pl.when(even[0] == 1)
+    def _():
+        fill(outer, inner)
+
+    @pl.when(even[0] == 0)
+    def _():
+        fill(inner, outer)
+
+
+def near_kernel(even, field, edge, first, noise, rest, out, middle, ends, sems):
+    def inside(start, here):
         for plane in (1, 2):
             along_z = field[plane + 1, here, :] + field[plane - 1, here, :]
             middle[plane - 1, here, :] = step(field, plane, start, along_z, KICK * noise[0, plane, here, :])
 
-    strips(body)
-
-    def fill(below, above):
-        below[0] = field[0]
-        below[1] = edge[0]
-        above[0] = field[3]
-        above[1] = edge[1]
+    def side(end, near, far):
+        def completed(start, here):
+            swept_end = edge[end // 3, here, :] + STEP_SIZE * first[0, here, :]
+            middle[2, here, :] = swept_end
+            inner = step(middle, near - 1, start, middle[far - 1, here, :], KICK * noise[1, near, here, :])
+            ends[1, here, :] = inner + STEP_SIZE * swept_end
+            rest[0, here, :] = middle[far - 1, here, :]
+            rest[1, here, :] = step(middle, far - 1, start, middle[near - 1, here, :], KICK * noise[1, far, here, :])
+
+        def last(start, here):
+            beyond = first[1, here, :] + STEP_SIZE * field[end, here, :]
+            along_z = middle[near - 1, here, :] + beyond
+            ends[0, here, :] = step(middle, 2, start, along_z, KICK * noise[1, end, here, :])
+
+        strips(completed)
+        inner_copy = pltpu.make_async_copy(ends.at[1], out.at[near], sems.at[1])
+        inner_copy.start()
+        strips(last)
+        end_copy = pltpu.make_async_copy(ends.at[0], out.at[end], sems.at[0])
+        end_copy.start()
+        inner_copy.wait()
+        end_copy.wait()
+
+    strips(inside)
 
     @pl.when(even[0] == 1)
     def _():
-        fill(outer, inner)
+        side(3, 2, 1)
 
     @pl.when(even[0] == 0)
     def _():
-        fill(inner, outer)
-
-
-def late_kernel(even, field, edge, first, second, middle, later, last, out, sides):
-    def near(below, above):
-        def body(start, here):
-            sides[0, here, :] = below[1, here, :] + STEP_SIZE * field[0, here, :] + middle[0, here, :]
-            sides[3, here, :] = above[1, here, :] + STEP_SIZE * field[3, here, :] + middle[1, here, :]
-            low = edge[0, here, :] + STEP_SIZE * below[0, here, :]
-            high = edge[1, here, :] + STEP_SIZE * above[0, here, :]
-            sides[1, here, :] = low
-            sides[2, here, :] = high
-            out[1, here, :] = later[0, here, :] + STEP_SIZE * low
-            out[2, here, :] = later[1, here, :] + STEP_SIZE * high
-
-        strips(body)
+        side(0, 1, 2)
+
+
+def far_kernel(even, field, edge, second, kicks, rest, started, out, whole, ends, sems):
+    def side(end, inner):
+        def completed(start, here):
+            swept_end = edge[end // 3, here, :] + STEP_SIZE * second[0, here, :]
+            whole[0, here, :] = swept_end
+            ends[1, here, :] = rest[1, here, :] + STEP_SIZE * swept_end
+
+        def last(start, here):
+            beyond = second[1, here, :] + STEP_SIZE * field[end, here, :]
+            ends[0, here, :] = step(whole, 0, start, rest[0, here, :] + beyond, KICK * kicks[end // 3, here, :])
+
+        strips(completed)
+        inner_copy = pltpu.make_async_copy(ends.at[1], out.at[inner], sems.at[1])
+        inner_copy.start()
+        strips(last)
+        end_copy = pltpu.make_async_copy(ends.at[0], out.at[end], sems.at[0])
+        end_copy.start()
+        inner_copy.wait()
+        end_copy.wait()
 
     @pl.when(even[0] == 1)
     def _():
-        near(second, first)
+        side(0, 1)
 
     @pl.when(even[0] == 0)
     def _():
-        near(first, second)
-
-    def end(start, here):
-        out[0, here, :] = step(sides, 1, start, sides[0, here, :], last[0, here, :])
-        out[3, here, :] = step(sides, 2, start, sides[3, here, :], last[1, here, :])
-
-    strips(end)
+        side(3, 2)
 
 
 def side_swap(turn, size):
@@ -163,14 +202,6 @@
             above = (slab + rep + turn) % 2 == 0
             pairs.append((rep * size + slab, rep * size + (slab + (1 if above else -1)) % size))
     return pairs
-
-
-def swept(center, along_z, kicks):
-    total = along_z + jnp.roll(center, -1, 1) + jnp.roll(center, 1, 1)
-    total = total + jnp.roll(center, -1, 2) + jnp.roll(center, 1, 2)
-    laplace = total - 6.0 * center
-    drift = laplace - MASS_TERM * center - COUPLING * center * center * center
-    return center + STEP_SIZE * drift + KICK * kicks
 
 
 def shards(phi_field, copy_counts, langevin_noise):
@@ -184,27 +215,38 @@
     even = ((lax.axis_index("slab") + lax.axis_index("rep")) % 2 == 0).astype(jnp.int32).reshape(1)
     pair = jax.ShapeDtypeStruct((2, height, width), jnp.float32)
     plane = 4 * height * width
-    edge, middle, inner, outer = pl.pallas_call(
+    edge, inner, outer = pl.pallas_call(
         edge_kernel,
-        out_shape=[pair] * 4,
+        out_shape=[pair] * 3,
         in_specs=[SMEM] + [VMEM] * 2,
-        out_specs=[VMEM] * 4,
+        out_specs=[VMEM] * 3,
         compiler_params=PARAMS,
         cost_estimate=cost(2 * 16 * plane // 4, 12 * plane),
     )(even, field, noise)
     first = lax.ppermute(inner, ("rep", "slab"), side_swap(0, size))
     second = lax.ppermute(outer, ("rep", "slab"), side_swap(1, size))
-    later = swept(middle, middle[::-1], noise[1, 1:3])
-    last = KICK * jnp.concatenate([noise[1, :1], noise[1, 3:]])
+    result = jax.ShapeDtypeStruct((planes, height, width), jnp.float32)
+    scratch = [pltpu.VMEM((2, height, width), jnp.float32), pltpu.SemaphoreType.DMA((2,))]
+    rest, out = pl.pallas_call(
+        near_kernel,
+        out_shape=[pair, result],
+        in_specs=[SMEM] + [VMEM] * 4,
+        out_specs=[VMEM, HBM],
+        scratch_shapes=[pltpu.VMEM((3, height, width), jnp.float32)] + scratch,
+        compiler_params=PARAMS,
+        cost_estimate=cost(5 * 16 * plane // 4, 20 * plane),
+    )(even, field, edge, first, noise)
+    kicks = jnp.concatenate([noise[1, :1], noise[1, 3:]])
     out = pl.pallas_call(
-        late_kernel,
-        out_shape=jax.ShapeDtypeStruct((planes, height, width), jnp.float32),
-        in_specs=[SMEM] + [VMEM] * 7,
-        out_specs=VMEM,
-        scratch_shapes=[pltpu.VMEM((4, height, width), jnp.float32)],
+        far_kernel,
+        out_shape=result,
+        in_specs=[SMEM] + [VMEM] * 5 + [HBM],
+        out_specs=HBM,
+        scratch_shapes=[pltpu.VMEM((1, height, width), jnp.float32)] + scratch,
+        input_output_aliases={6: 0},
         compiler_params=PARAMS,
-        cost_estimate=cost(3 * 16 * plane // 4, 20 * plane),
-    )(even, field, edge, first, second, middle, later, last)
+        cost_estimate=cost(16 * plane // 4, 10 * plane),
+    )(even, field, edge, second, kicks, rest, out)
     return out[None]
 
 

time: 112 us -> 107 us (0.955)
  the two profiles are of different devices: /device:TPU:72 before, /device:TPU:68 now
where the time goes in v4:
time: 107 us
  waiting for transfers between devices  64.4 us (60%)
  starting transfers between devices  28.2 us (26%)
  between operations  4.81 us (4%)
  Pallas kernels  4.46 us (4%)
  other arithmetic  3.71 us (3%)
  local copies, waits for them, and re-layouts  1.24 us (1%)
    all_to_all x2, waiting for transfers between devices, exchange(): lax.all_to_all(parts, 'rep', split_axis=0, concat_axis=0, tiled=True, axi...  46.5 us
    all_to_all x2, starting transfers between devices, exchange(): lax.all_to_all(parts, 'rep', split_axis=0, concat_axis=0, tiled=True, axi...  13.1 us
    ppermute x1, waiting for transfers between devices, shards(): first = lax.ppermute(inner, ('rep', 'slab'), side_swap(0, size))  11.3 us
    ppermute x1, starting transfers between devices, crossing(): lax.ppermute(jnp.take(spread, send[:width], axis=0, mode='clip'), 'rep',...  10 us
    ppermute x1, waiting for transfers between devices, crossing(): lax.ppermute(jnp.take(spread, send[:width], axis=0, mode='clip'), 'rep',...  6.68 us
    ppermute x1, starting transfers between devices, shards(): first = lax.ppermute(inner, ('rep', 'slab'), side_swap(0, size))  3.1 us
    pallas_call x1, Pallas kernels, shards(): pl.pallas_call(near_kernel, out_shape=[pair, result], in_specs=[SMEM] + [...  2.5 us
  transfers between devices with their start and end apart: 5, of which 4 were waited for; matrix products, arithmetic and copies ran while one was open for 3% of the time, Pallas kernels for 2%

profile of v4, /device:TPU:68, one launch (start us, length us, event | category | flops | bytes accessed | tf_op | source)
XLA Modules:
  0.0 106.9 jit_solution(2434091590120589253)
XLA Ops:
  0.0 0.0 copy-start.3
  0.0 0.0 copy-start.2
  0.0 7.3 %all-to-all-start = ((f32[16,64,256]{2,1,0:T(8,128)}), f32[16,64,256]{2,1,0:T(8,128)S(1)}, u32[]{:S(2)}, u32[]{:S(2)}) async-start(f32[16,64,256]{2,1,0:T(8,128)} %bitcast.90), calls=%async_computation | async-start | bytes 2097152 | tf_op jit(solution)/shard_map/all_to_all | solution.py:32
  7.4 0.0 copy-done.1
  7.4 0.1 select_reduce_fusion
  7.5 0.1 select_reduce_fusion.1
  7.6 0.2 convert_reduce_fusion.1
  7.8 0.1 fusion.1
  7.9 0.6 convert_reduce_fusion.2
  11.2 0.7 slice_reduce_fusion
  13.9 0.1 convert_reduce_fusion
  14.0 0.0 copy-done.3
  14.1 0.2 select_reduce_fusion.4
  14.2 0.0 copy-done.2
  14.3 0.2 select_reduce_fusion.2
  14.5 19.7 %all-to-all-done = f32[16,64,256]{2,1,0:T(8,128)S(1)} async-done(((f32[16,64,256]{2,1,0:T(8,128)}), f32[16,64,256]{2,1,0:T(8,128)S(1)}, u32[]{:S(2)}, u32[]{:S(2)}) %all-to-all-start) | async-done | bytes 1048608 | tf_op jit(solution)/shard_map/all_to_all | solution.py:32
  34.2 19.2 %conditional.1 = (f32[16,64,256]{2,1,0:T(8,128)}) conditional(s32[]{:T(128)} %clamp.3, (s32[16]{0:T(128)S(1)}, f32[16,64,256]{2,1,0:T(8,128)S(1)}) %tuple.44, (s32[16]{0:T(128)S(1)}, s32[16]{0:T(128)S(1)}, f32[16,64,256]{2,1,0:T(8,128)S(1)}) %tuple.45, (s32[16]{0:T(128)S(1)}, s32[16]{0:T(128)S(1)}, ...), branch_computations={%region_10.11_spmd, %region_11.12_spmd, %region_12.13_spmd, %regio... | conditional | flops 1575008 | bytes 12591408 | solution.py:84
  34.2 0.6 gather_fusion.3
  34.7 10.0 %collective-permute-start.1 = (f32[3,64,256]{2,1,0:T(8,128)S(1)}, f32[3,64,256]{2,1,0:T(8,128)S(1)}, u32[]{:S(2)}, u32[]{:S(2)}) collective-permute-start(f32[3,64,256]{2,1,0:T(8,128)S(1)} %gather_fusion.3), channel_id=1, source_target_pairs={{0,256},{16,272},{32,288},{48,304},{64,320},{80,336},{96,352},{112... | collective-permute-start | bytes 589832 | tf_op jit(solution)/shard_map/cond/branch_3_fun/ppermute | solution.py:72
  44.8 0.6 gather_fusion.4
  45.4 6.7 %collective-permute-done.1 = f32[3,64,256]{2,1,0:T(8,128)S(1)} collective-permute-done((f32[3,64,256]{2,1,0:T(8,128)S(1)}, f32[3,64,256]{2,1,0:T(8,128)S(1)}, u32[]{:S(2)}, u32[]{:S(2)}) %collective-permute-start.1) | collective-permute-done | bytes 196640 | tf_op jit(solution)/shard_map/cond/branch_3_fun/ppermute | solution.py:72
  52.1 1.3 %select_select_fusion.1 = f32[16,64,256]{2,1,0:T(8,128)} fusion(f32[16,64,256]{2,1,0:T(8,128)S(1)} %gather_fusion.4, f32[64,256]{1,0:T(8,128)S(1)} %get-tuple-element.172, f32[64,256]{1,0:T(8,128)S(1)} %get-tuple-element.173, f32[64,256]{1,0:T(8,128)S(1)} %get-tuple-element.171, pred[16]{0:T(512)(128)(4,1)S(1)} %get-tuple-element.175, ...), kind=kLoop, calls=%fused_computation.31 | loop fusion | flops 786432 | bytes 2293808 | tf_op jit(solution)/shard_map/cond/branch_3_fun/jit(_where)/select_n | solution.py:77
  53.4 5.8 %all-to-all-start.1 = ((f32[16,64,256]{2,1,0:T(8,128)}), f32[16,64,256]{2,1,0:T(8,128)S(1)}, u32[]{:S(2)}, u32[]{:S(2)}) async-start(f32[16,64,256]{2,1,0:T(8,128)} %get-tuple-element.233), calls=%async_computation.1 | async-start | bytes 2097152 | tf_op jit(solution)/shard_map/all_to_all | solution.py:32
  59.2 26.8 %all-to-all-done.1 = f32[16,64,256]{2,1,0:T(8,128)S(1)} async-done(((f32[16,64,256]{2,1,0:T(8,128)}), f32[16,64,256]{2,1,0:T(8,128)S(1)}, u32[]{:S(2)}, u32[]{:S(2)}) %all-to-all-start.1) | async-done | bytes 1048608 | tf_op jit(solution)/shard_map/all_to_all | solution.py:32
  86.0 0.0 copy-done
  86.0 0.7 shard_map.55
  86.7 3.1 %collective-permute-start.13 = (f32[2,256,256]{2,1,0:T(8,128)S(1)}, f32[2,256,256]{2,1,0:T(8,128)S(1)}, u32[]{:S(2)}, u32[]{:S(2)}) collective-permute-start(f32[2,256,256]{2,1,0:T(8,128)S(1)} %get-tuple-element.140), channel_id=1, source_target_pairs={{0,1},{1,0},{2,3},{3,2},{4,5},{5,4},{6,7},{7,6},{8,9},{9,8},{10,11... | collective-permute-start | bytes 1572872 | tf_op jit(solution)/shard_map/ppermute | solution.py:226
  89.8 1.9 %collective-permute-start.12 = (f32[2,256,256]{2,1,0:T(8,128)S(1)}, f32[2,256,256]{2,1,0:T(8,128)S(1)}, u32[]{:S(2)}, u32[]{:S(2)}) collective-permute-start(f32[2,256,256]{2,1,0:T(8,128)S(1)} %get-tuple-element.139), channel_id=1, source_target_pairs={{0,15},{1,2},{2,1},{3,4},{4,3},{5,6},{6,5},{7,8},{8,7},{9,10},{10,... | collective-permute-start | bytes 1572872 | tf_op jit(solution)/shard_map/ppermute | solution.py:227
  91.8 11.3 %collective-permute-done.13.first = f32[2,256,256]{2,1,0:T(8,128)S(1)} collective-permute-done((f32[2,256,256]{2,1,0:T(8,128)S(1)}, f32[2,256,256]{2,1,0:T(8,128)S(1)}, u32[]{:S(2)}, u32[]{:S(2)}) %collective-permute-start.13) | collective-permute-done | bytes 524320 | tf_op jit(solution)/shard_map/ppermute | solution.py:226
  103.0 2.5 %shard_map.56 = (f32[2,256,256]{2,1,0:T(8,128)S(1)}, f32[4,256,256]{2,1,0:T(8,128)}) custom-call(s32[1]{0:T(128)} %bitcast.34.even, f32[4,256,256]{2,1,0:T(8,128)S(1)} %bitcast.85, f32[2,256,256]{2,1,0:T(8,128)S(1)} %get-tuple-element.138.edge, f32[2,256,256]{2,1,0:T(8,128)S(1)} %collective-permute-done.13.first, f32[2,4,256,256]{3,2,1,0:T(8,128)S(1)} %bitcast.89), custom_call_target="tpu_custom_call" | custom-call | flops 5242880 | bytes 5242880 | tf_op jit(solution)/shard_map/pallas_call | solution.py:230
  105.5 0.0 collective-permute-done.12.second
  105.5 1.3 %shard_map.57 = f32[4,256,256]{2,1,0:T(8,128)} custom-call(s32[1]{0:T(128)} %bitcast.34.even, f32[4,256,256]{2,1,0:T(8,128)S(1)} %bitcast.86, f32[2,256,256]{2,1,0:T(8,128)S(1)} %get-tuple-element.138.edge, f32[2,256,256]{2,1,0:T(8,128)S(1)} %collective-permute-done.12.second, ...), custom_call_target="tpu_custom_call", output_to_operand_aliasing={{}: (6, {})} | custom-call | flops 1048576 | bytes 2621440 | tf_op jit(solution)/shard_map/pallas_call | solution.py:240
  (15 shorter events, 0.2 us)
Async XLA Ops:
  0.0 14.0 %copy-start.3 = (s32[16]{0:T(128)S(1)}, s32[16]{0:T(128)}, u32[]{:S(2)}) copy-start(s32[16]{0:T(128)} %constant.145.clone) | copy-start | bytes 196
  0.0 14.2 %copy-start.2 = (s32[32]{0:T(128)S(1)}, s32[32]{0:T(128)}, u32[]{:S(2)}) copy-start(s32[32]{0:T(128)} %constant.144.clone) | copy-start | bytes 388
  0.0 7.4 %copy-start.1 = (s32[32]{0:T(128)S(1)}, s32[32]{0:T(128)}, u32[]{:S(2)}) copy-start(s32[32]{0:T(128)} %param.19) | copy-start | bytes 388
  0.0 34.2 %all-to-all-start = ((f32[16,64,256]{2,1,0:T(8,128)}), f32[16,64,256]{2,1,0:T(8,128)S(1)}, u32[]{:S(2)}, u32[]{:S(2)}) async-start(f32[16,64,256]{2,1,0:T(8,128)} %bitcast.90), calls=%async_computation | async-start | bytes 2097152 | tf_op jit(solution)/shard_map/all_to_all | solution.py:32
  34.7 17.4 %collective-permute-start.1 = (f32[3,64,256]{2,1,0:T(8,128)S(1)}, f32[3,64,256]{2,1,0:T(8,128)S(1)}, u32[]{:S(2)}, u32[]{:S(2)}) collective-permute-start(f32[3,64,256]{2,1,0:T(8,128)S(1)} %gather_fusion.3), channel_id=1, source_target_pairs={{0,256},{16,272},{32,288},{48,304},{64,320},{80,336},{96,352},{112... | collective-permute-start | bytes 589832 | tf_op jit(solution)/shard_map/cond/branch_3_fun/ppermute | solution.py:72
  53.4 32.6 %copy-start = (f32[2,1,4,256,256]{4,3,2,1,0:T(8,128)S(1)}, f32[2,1,4,256,256]{4,3,2,1,0:T(8,128)}, u32[]{:S(2)}) copy-start(f32[2,1,4,256,256]{4,3,2,1,0:T(8,128)} %param.20) | copy-start | bytes 6291460
  53.4 32.6 %all-to-all-start.1 = ((f32[16,64,256]{2,1,0:T(8,128)}), f32[16,64,256]{2,1,0:T(8,128)S(1)}, u32[]{:S(2)}, u32[]{:S(2)}) async-start(f32[16,64,256]{2,1,0:T(8,128)} %get-tuple-element.233), calls=%async_computation.1 | async-start | bytes 2097152 | tf_op jit(solution)/shard_map/all_to_all | solution.py:32
  86.7 16.4 %collective-permute-start.13 = (f32[2,256,256]{2,1,0:T(8,128)S(1)}, f32[2,256,256]{2,1,0:T(8,128)S(1)}, u32[]{:S(2)}, u32[]{:S(2)}) collective-permute-start(f32[2,256,256]{2,1,0:T(8,128)S(1)} %get-tuple-element.140), channel_id=1, source_target_pairs={{0,1},{1,0},{2,3},{3,2},{4,5},{5,4},{6,7},{7,6},{8,9},{9,8},{10,11... | collective-permute-start | bytes 1572872 | tf_op jit(solution)/shard_map/ppermute | solution.py:226
  89.8 15.8 %collective-permute-start.12 = (f32[2,256,256]{2,1,0:T(8,128)S(1)}, f32[2,256,256]{2,1,0:T(8,128)S(1)}, u32[]{:S(2)}, u32[]{:S(2)}) collective-permute-start(f32[2,256,256]{2,1,0:T(8,128)S(1)} %get-tuple-element.139), channel_id=1, source_target_pairs={{0,15},{1,2},{2,1},{3,4},{4,3},{5,6},{6,5},{7,8},{8,7},{9,10},{10,... | collective-permute-start | bytes 1572872 | tf_op jit(solution)/shard_map/ppermute | solution.py:227

commit v5 on v4

--- a/solution.py
+++ b/solution.py
@@ -12,7 +12,7 @@
 COUPLING = 0.5
 KICK = (2.0 * STEP_SIZE) ** 0.5
 HALF = 16
-STRIP = 64
+STRIP = 128
 VMEM = pl.BlockSpec(memory_space=pltpu.VMEM)
 SMEM = pl.BlockSpec(memory_space=pltpu.SMEM)
 HBM = pl.BlockSpec(memory_space=pl.ANY)

time: 107 us -> 104 us (0.972)
  the two profiles are of different devices: /device:TPU:68 before, /device:TPU:78 now
where the time goes in v5:
time: 104 us; the launch traced here: 103 us
  waiting for transfers between devices  61.4 us (59%)
  starting transfers between devices  28.6 us (28%)
  between operations  4.75 us (5%)
  Pallas kernels  3.79 us (4%)
  other arithmetic  3.6 us (3%)
  local copies, waits for them, and re-layouts  1.23 us (1%)
    all_to_all x2, waiting for transfers between devices, exchange(): lax.all_to_all(parts, 'rep', split_axis=0, concat_axis=0, tiled=True, axi...  46.1 us
    all_to_all x2, starting transfers between devices, exchange(): lax.all_to_all(parts, 'rep', split_axis=0, concat_axis=0, tiled=True, axi...  11.9 us
    ppermute x1, starting transfers between devices, crossing(): lax.ppermute(jnp.take(spread, send[:width], axis=0, mode='clip'), 'rep',...  10 us
    ppermute x1, waiting for transfers between devices, shards(): first = lax.ppermute(inner, ('rep', 'slab'), side_swap(0, size))  7.12 us
    ppermute x1, waiting for transfers between devices, crossing(): lax.ppermute(jnp.take(spread, send[:width], axis=0, mode='clip'), 'rep',...  5.75 us
    ppermute x1, starting transfers between devices, shards(): second = lax.ppermute(outer, ('rep', 'slab'), side_swap(1, size))  3.93 us
    ppermute x1, starting transfers between devices, shards(): first = lax.ppermute(inner, ('rep', 'slab'), side_swap(0, size))  2.75 us
    ppermute x1, waiting for transfers between devices, shards(): second = lax.ppermute(outer, ('rep', 'slab'), side_swap(1, size))  2.5 us
  transfers between devices with their start and end apart: 5, of which 5 were waited for; matrix products, arithmetic and copies ran while one was open for 3% of the time, Pallas kernels for 2%

profile of v5, /device:TPU:78, one launch (start us, length us, event | category | flops | bytes accessed | tf_op | source)
XLA Modules:
  0.0 103.4 jit_solution(17992256531569874059)
XLA Ops:
  0.0 0.0 copy-start.3
  0.0 0.0 copy-start.2
  0.0 7.7 %all-to-all-start = ((f32[16,64,256]{2,1,0:T(8,128)}), f32[16,64,256]{2,1,0:T(8,128)S(1)}, u32[]{:S(2)}, u32[]{:S(2)}) async-start(f32[16,64,256]{2,1,0:T(8,128)} %bitcast.90), calls=%async_computation | async-start | bytes 2097152 | tf_op jit(solution)/shard_map/all_to_all | solution.py:32
  7.7 0.0 copy-done.1
  7.7 0.1 select_reduce_fusion
  7.9 0.1 select_reduce_fusion.1
  8.0 0.2 convert_reduce_fusion.1
  8.2 0.1 fusion.1
  8.3 0.6 convert_reduce_fusion.2
  11.5 0.7 slice_reduce_fusion
  14.3 0.1 convert_reduce_fusion
  14.4 0.0 copy-done.3
  14.4 0.2 select_reduce_fusion.4
  14.6 0.0 copy-done.2
  14.6 0.2 select_reduce_fusion.2
  14.8 19.5 %all-to-all-done = f32[16,64,256]{2,1,0:T(8,128)S(1)} async-done(((f32[16,64,256]{2,1,0:T(8,128)}), f32[16,64,256]{2,1,0:T(8,128)S(1)}, u32[]{:S(2)}, u32[]{:S(2)}) %all-to-all-start) | async-done | bytes 1048608 | tf_op jit(solution)/shard_map/all_to_all | solution.py:32
  34.3 18.2 %conditional.1 = (f32[16,64,256]{2,1,0:T(8,128)}) conditional(s32[]{:T(128)} %clamp.3, (s32[16]{0:T(128)S(1)}, f32[16,64,256]{2,1,0:T(8,128)S(1)}) %tuple.44, (s32[16]{0:T(128)S(1)}, s32[16]{0:T(128)S(1)}, f32[16,64,256]{2,1,0:T(8,128)S(1)}) %tuple.45, (s32[16]{0:T(128)S(1)}, s32[16]{0:T(128)S(1)}, ...), branch_computations={%region_10.11_spmd, %region_11.12_spmd, %region_12.13_spmd, %regio... | conditional | flops 1575008 | bytes 12591408 | solution.py:84
  34.3 0.6 gather_fusion.1
  34.9 10.0 %collective-permute-start = (f32[2,64,256]{2,1,0:T(8,128)S(1)}, f32[2,64,256]{2,1,0:T(8,128)S(1)}, u32[]{:S(2)}, u32[]{:S(2)}) collective-permute-start(f32[2,64,256]{2,1,0:T(8,128)S(1)} %gather_fusion.1), channel_id=1, source_target_pairs={{0,256},{16,272},{32,288},{48,304},{64,320},{80,336},{96,352},{112... | collective-permute-start | bytes 393224 | tf_op jit(solution)/shard_map/cond/branch_2_fun/ppermute | solution.py:72
  44.9 0.6 gather_fusion.2
  45.5 5.7 %collective-permute-done = f32[2,64,256]{2,1,0:T(8,128)S(1)} collective-permute-done((f32[2,64,256]{2,1,0:T(8,128)S(1)}, f32[2,64,256]{2,1,0:T(8,128)S(1)}, u32[]{:S(2)}, u32[]{:S(2)}) %collective-permute-start) | collective-permute-done | bytes 131104 | tf_op jit(solution)/shard_map/cond/branch_2_fun/ppermute | solution.py:72
  51.3 1.2 %select_select_fusion = f32[16,64,256]{2,1,0:T(8,128)} fusion(f32[16,64,256]{2,1,0:T(8,128)S(1)} %gather_fusion.2, f32[64,256]{1,0:T(8,128)S(1)} %get-tuple-element.168, f32[64,256]{1,0:T(8,128)S(1)} %get-tuple-element.167, pred[16]{0:T(512)(128)(4,1)S(1)} %get-tuple-element.170, pred[16]{0:T(512)(128)(4,1)S(1)} %get-tuple-element.169), kind=kLoop, calls=%fused_computation.24 | loop fusion | flops 524288 | bytes 2228256 | tf_op jit(solution)/shard_map/cond/branch_2_fun/jit(_where)/select_n | solution.py:77
  52.5 4.2 %all-to-all-start.1 = ((f32[16,64,256]{2,1,0:T(8,128)}), f32[16,64,256]{2,1,0:T(8,128)S(1)}, u32[]{:S(2)}, u32[]{:S(2)}) async-start(f32[16,64,256]{2,1,0:T(8,128)} %get-tuple-element.233), calls=%async_computation.1 | async-start | bytes 2097152 | tf_op jit(solution)/shard_map/all_to_all | solution.py:32
  56.6 26.6 %all-to-all-done.1 = f32[16,64,256]{2,1,0:T(8,128)S(1)} async-done(((f32[16,64,256]{2,1,0:T(8,128)}), f32[16,64,256]{2,1,0:T(8,128)S(1)}, u32[]{:S(2)}, u32[]{:S(2)}) %all-to-all-start.1) | async-done | bytes 1048608 | tf_op jit(solution)/shard_map/all_to_all | solution.py:32
  83.2 0.0 copy-done
  83.2 0.5 shard_map.55
  83.7 2.7 %collective-permute-start.13 = (f32[2,256,256]{2,1,0:T(8,128)S(1)}, f32[2,256,256]{2,1,0:T(8,128)S(1)}, u32[]{:S(2)}, u32[]{:S(2)}) collective-permute-start(f32[2,256,256]{2,1,0:T(8,128)S(1)} %get-tuple-element.140), channel_id=1, source_target_pairs={{0,1},{1,0},{2,3},{3,2},{4,5},{5,4},{6,7},{7,6},{8,9},{9,8},{10,11... | collective-permute-start | bytes 1572872 | tf_op jit(solution)/shard_map/ppermute | solution.py:226
  86.5 3.9 %collective-permute-start.12 = (f32[2,256,256]{2,1,0:T(8,128)S(1)}, f32[2,256,256]{2,1,0:T(8,128)S(1)}, u32[]{:S(2)}, u32[]{:S(2)}) collective-permute-start(f32[2,256,256]{2,1,0:T(8,128)S(1)} %get-tuple-element.139), channel_id=1, source_target_pairs={{0,15},{1,2},{2,1},{3,4},{4,3},{5,6},{6,5},{7,8},{8,7},{9,10},{10,... | collective-permute-start | bytes 1572872 | tf_op jit(solution)/shard_map/ppermute | solution.py:227
  90.5 7.1 %collective-permute-done.13.first = f32[2,256,256]{2,1,0:T(8,128)S(1)} collective-permute-done((f32[2,256,256]{2,1,0:T(8,128)S(1)}, f32[2,256,256]{2,1,0:T(8,128)S(1)}, u32[]{:S(2)}, u32[]{:S(2)}) %collective-permute-start.13) | collective-permute-done | bytes 524320 | tf_op jit(solution)/shard_map/ppermute | solution.py:226
  97.6 2.1 %shard_map.56 = (f32[2,256,256]{2,1,0:T(8,128)S(1)}, f32[4,256,256]{2,1,0:T(8,128)}) custom-call(s32[1]{0:T(128)} %bitcast.34.even, f32[4,256,256]{2,1,0:T(8,128)S(1)} %bitcast.85, f32[2,256,256]{2,1,0:T(8,128)S(1)} %get-tuple-element.138.edge, f32[2,256,256]{2,1,0:T(8,128)S(1)} %collective-permute-done.13.first, f32[2,4,256,256]{3,2,1,0:T(8,128)S(1)} %bitcast.89), custom_call_target="tpu_custom_call" | custom-call | flops 5242880 | bytes 5242880 | tf_op jit(solution)/shard_map/pallas_call | solution.py:230
  99.8 2.5 %collective-permute-done.12.second = f32[2,256,256]{2,1,0:T(8,128)S(1)} collective-permute-done((f32[2,256,256]{2,1,0:T(8,128)S(1)}, f32[2,256,256]{2,1,0:T(8,128)S(1)}, u32[]{:S(2)}, u32[]{:S(2)}) %collective-permute-start.12) | collective-permute-done | bytes 524320 | tf_op jit(solution)/shard_map/ppermute | solution.py:227
  102.3 1.1 %shard_map.57 = f32[4,256,256]{2,1,0:T(8,128)} custom-call(s32[1]{0:T(128)} %bitcast.34.even, f32[4,256,256]{2,1,0:T(8,128)S(1)} %bitcast.86, f32[2,256,256]{2,1,0:T(8,128)S(1)} %get-tuple-element.138.edge, f32[2,256,256]{2,1,0:T(8,128)S(1)} %collective-permute-done.12.second, ...), custom_call_target="tpu_custom_call", output_to_operand_aliasing={{}: (6, {})} | custom-call | flops 1048576 | bytes 2621440 | tf_op jit(solution)/shard_map/pallas_call | solution.py:240
  (15 shorter events, 0.2 us)
Async XLA Ops:
  0.0 14.4 %copy-start.3 = (s32[16]{0:T(128)S(1)}, s32[16]{0:T(128)}, u32[]{:S(2)}) copy-start(s32[16]{0:T(128)} %constant.145.clone) | copy-start | bytes 196
  0.0 14.6 %copy-start.2 = (s32[32]{0:T(128)S(1)}, s32[32]{0:T(128)}, u32[]{:S(2)}) copy-start(s32[32]{0:T(128)} %constant.144.clone) | copy-start | bytes 388
  0.0 7.7 %copy-start.1 = (s32[32]{0:T(128)S(1)}, s32[32]{0:T(128)}, u32[]{:S(2)}) copy-start(s32[32]{0:T(128)} %param.19) | copy-start | bytes 388
  0.0 34.3 %all-to-all-start = ((f32[16,64,256]{2,1,0:T(8,128)}), f32[16,64,256]{2,1,0:T(8,128)S(1)}, u32[]{:S(2)}, u32[]{:S(2)}) async-start(f32[16,64,256]{2,1,0:T(8,128)} %bitcast.90), calls=%async_computation | async-start | bytes 2097152 | tf_op jit(solution)/shard_map/all_to_all | solution.py:32
  34.9 16.4 %collective-permute-start = (f32[2,64,256]{2,1,0:T(8,128)S(1)}, f32[2,64,256]{2,1,0:T(8,128)S(1)}, u32[]{:S(2)}, u32[]{:S(2)}) collective-permute-start(f32[2,64,256]{2,1,0:T(8,128)S(1)} %gather_fusion.1), channel_id=1, source_target_pairs={{0,256},{16,272},{32,288},{48,304},{64,320},{80,336},{96,352},{112... | collective-permute-start | bytes 393224 | tf_op jit(solution)/shard_map/cond/branch_2_fun/ppermute | solution.py:72
  52.5 30.7 %copy-start = (f32[2,1,4,256,256]{4,3,2,1,0:T(8,128)S(1)}, f32[2,1,4,256,256]{4,3,2,1,0:T(8,128)}, u32[]{:S(2)}) copy-start(f32[2,1,4,256,256]{4,3,2,1,0:T(8,128)} %param.20) | copy-start | bytes 6291460
  52.5 30.7 %all-to-all-start.1 = ((f32[16,64,256]{2,1,0:T(8,128)}), f32[16,64,256]{2,1,0:T(8,128)S(1)}, u32[]{:S(2)}, u32[]{:S(2)}) async-start(f32[16,64,256]{2,1,0:T(8,128)} %get-tuple-element.233), calls=%async_computation.1 | async-start | bytes 2097152 | tf_op jit(solution)/shard_map/all_to_all | solution.py:32
  83.7 13.9 %collective-permute-start.13 = (f32[2,256,256]{2,1,0:T(8,128)S(1)}, f32[2,256,256]{2,1,0:T(8,128)S(1)}, u32[]{:S(2)}, u32[]{:S(2)}) collective-permute-start(f32[2,256,256]{2,1,0:T(8,128)S(1)} %get-tuple-element.140), channel_id=1, source_target_pairs={{0,1},{1,0},{2,3},{3,2},{4,5},{5,4},{6,7},{7,6},{8,9},{9,8},{10,11... | collective-permute-start | bytes 1572872 | tf_op jit(solution)/shard_map/ppermute | solution.py:226
  86.5 15.8 %collective-permute-start.12 = (f32[2,256,256]{2,1,0:T(8,128)S(1)}, f32[2,256,256]{2,1,0:T(8,128)S(1)}, u32[]{:S(2)}, u32[]{:S(2)}) collective-permute-start(f32[2,256,256]{2,1,0:T(8,128)S(1)} %get-tuple-element.139), channel_id=1, source_target_pairs={{0,15},{1,2},{2,1},{3,4},{4,3},{5,6},{6,5},{7,8},{8,7},{9,10},{10,... | collective-permute-start | bytes 1572872 | tf_op jit(solution)/shard_map/ppermute | solution.py:227

commit v6 on v5

--- a/solution.py
+++ b/solution.py
@@ -103,30 +103,26 @@
         body(start, pl.ds(start, STRIP))
 
 
-def edge_kernel(even, field, noise, edge, inner, outer):
-    def fill(below, above):
+def edge_kernel(above, field, noise, *refs):
+    sent = refs[-1]
+
+    def fill(plane, inward):
         def body(start, here):
-            low = step(field, 0, start, field[1, here, :], KICK * noise[0, 0, here, :])
-            high = step(field, 3, start, field[2, here, :], KICK * noise[0, 3, here, :])
-            edge[0, here, :] = low
-            edge[1, here, :] = high
-            below[0, here, :] = field[0, here, :]
-            below[1, here, :] = low
-            above[0, here, :] = field[3, here, :]
-            above[1, here, :] = high
+            sent[0, here, :] = field[plane, here, :]
+            sent[1, here, :] = step(field, plane, start, field[inward, here, :], KICK * noise[0, plane, here, :])
 
         strips(body)
 
-    @pl.when(even[0] == 1)
-    def _():
-        fill(outer, inner)
-
-    @pl.when(even[0] == 0)
-    def _():
-        fill(inner, outer)
-
-
-def near_kernel(even, field, edge, first, noise, rest, out, middle, ends, sems):
+    @pl.when(above[0] == 1)
+    def _():
+        fill(3, 2)
+
+    @pl.when(above[0] == 0)
+    def _():
+        fill(0, 1)
+
+
+def near_kernel(even, field, sent, first, noise, rest, out, middle, ends, sems):
     def inside(start, here):
         for plane in (1, 2):
             along_z = field[plane + 1, here, :] + field[plane - 1, here, :]
@@ -134,7 +130,7 @@
 
     def side(end, near, far):
         def completed(start, here):
-            swept_end = edge[end // 3, here, :] + STEP_SIZE * first[0, here, :]
+            swept_end = sent[1, here, :] + STEP_SIZE * first[0, here, :]
             middle[2, here, :] = swept_end
             inner = step(middle, near - 1, start, middle[far - 1, here, :], KICK * noise[1, near, here, :])
             ends[1, here, :] = inner + STEP_SIZE * swept_end
@@ -142,7 +138,7 @@
             rest[1, here, :] = step(middle, far - 1, start, middle[near - 1, here, :], KICK * noise[1, far, here, :])
 
         def last(start, here):
-            beyond = first[1, here, :] + STEP_SIZE * field[end, here, :]
+            beyond = first[1, here, :] + STEP_SIZE * sent[0, here, :]
             along_z = middle[near - 1, here, :] + beyond
             ends[0, here, :] = step(middle, 2, start, along_z, KICK * noise[1, end, here, :])
 
@@ -166,15 +162,15 @@
         side(0, 1, 2)
 
 
-def far_kernel(even, field, edge, second, kicks, rest, started, out, whole, ends, sems):
+def far_kernel(even, sent, second, kicks, rest, started, out, whole, ends, sems):
     def side(end, inner):
         def completed(start, here):
-            swept_end = edge[end // 3, here, :] + STEP_SIZE * second[0, here, :]
+            swept_end = sent[1, here, :] + STEP_SIZE * second[0, here, :]
             whole[0, here, :] = swept_end
             ends[1, here, :] = rest[1, here, :] + STEP_SIZE * swept_end
 
         def last(start, here):
-            beyond = second[1, here, :] + STEP_SIZE * field[end, here, :]
+            beyond = second[1, here, :] + STEP_SIZE * sent[0, here, :]
             ends[0, here, :] = step(whole, 0, start, rest[0, here, :] + beyond, KICK * kicks[end // 3, here, :])
 
         strips(completed)
@@ -215,14 +211,18 @@
     even = ((lax.axis_index("slab") + lax.axis_index("rep")) % 2 == 0).astype(jnp.int32).reshape(1)
     pair = jax.ShapeDtypeStruct((2, height, width), jnp.float32)
     plane = 4 * height * width
-    edge, inner, outer = pl.pallas_call(
-        edge_kernel,
-        out_shape=[pair] * 3,
-        in_specs=[SMEM] + [VMEM] * 2,
-        out_specs=[VMEM] * 3,
-        compiler_params=PARAMS,
-        cost_estimate=cost(2 * 16 * plane // 4, 12 * plane),
-    )(even, field, noise)
+    def made(above, *after):
+        return pl.pallas_call(
+            edge_kernel,
+            out_shape=pair,
+            in_specs=[SMEM] + [VMEM] * 2 + [HBM] * len(after),
+            out_specs=VMEM,
+            compiler_params=PARAMS,
+            cost_estimate=cost(16 * plane // 4, 5 * plane),
+        )(above, field, noise, *after)
+
+    inner = made(even)
+    outer = made(1 - even, inner)
     first = lax.ppermute(inner, ("rep", "slab"), side_swap(0, size))
     second = lax.ppermute(outer, ("rep", "slab"), side_swap(1, size))
     result = jax.ShapeDtypeStruct((planes, height, width), jnp.float32)
@@ -235,18 +235,18 @@
         scratch_shapes=[pltpu.VMEM((3, height, width), jnp.float32)] + scratch,
         compiler_params=PARAMS,
         cost_estimate=cost(5 * 16 * plane // 4, 20 * plane),
-    )(even, field, edge, first, noise)
+    )(even, field, inner, first, noise)
     kicks = jnp.concatenate([noise[1, :1], noise[1, 3:]])
     out = pl.pallas_call(
         far_kernel,
         out_shape=result,
-        in_specs=[SMEM] + [VMEM] * 5 + [HBM],
+        in_specs=[SMEM] + [VMEM] * 4 + [HBM],
         out_specs=HBM,
         scratch_shapes=[pltpu.VMEM((1, height, width), jnp.float32)] + scratch,
-        input_output_aliases={6: 0},
+        input_output_aliases={5: 0},
         compiler_params=PARAMS,
         cost_estimate=cost(16 * plane // 4, 10 * plane),
-    )(even, field, edge, second, kicks, rest, out)
+    )(even, outer, second, kicks, rest, out)
     return out[None]
 
 

time: 104 us -> 92.2 us (0.89)
  the two profiles are of different devices: /device:TPU:78 before, /device:TPU:8 now
where the time goes in v6:
time: 92.2 us; the launch traced here: 91.8 us
  waiting for transfers between devices  53.9 us (58%)
  starting transfers between devices  25.3 us (27%)
  between operations  4.72 us (5%)
  Pallas kernels  3.96 us (4%)
  other arithmetic  2.34 us (3%)
  local copies, waits for them, and re-layouts  1.64 us (2%)
    all_to_all x2, waiting for transfers between devices, exchange(): lax.all_to_all(parts, 'rep', split_axis=0, concat_axis=0, tiled=True, axi...  46.4 us
    all_to_all x2, starting transfers between devices, exchange(): lax.all_to_all(parts, 'rep', split_axis=0, concat_axis=0, tiled=True, axi...  14.2 us
    ppermute x1, starting transfers between devices, shards(): second = lax.ppermute(outer, ('rep', 'slab'), side_swap(1, size))  9.15 us
    ppermute x1, waiting for transfers between devices, shards(): second = lax.ppermute(outer, ('rep', 'slab'), side_swap(1, size))  7.42 us
    pallas_call x1, Pallas kernels, shards(): pl.pallas_call(near_kernel, out_shape=[pair, result], in_specs=[SMEM] + [...  2.13 us
    ppermute x1, starting transfers between devices, shards(): first = lax.ppermute(inner, ('rep', 'slab'), side_swap(0, size))  1.92 us
  transfers between devices with their start and end apart: 4, of which 3 were waited for; matrix products, arithmetic and copies ran while one was open for 3% of the time, Pallas kernels for 3%

profile of v6, /device:TPU:8, one launch (start us, length us, event | category | flops | bytes accessed | tf_op | source)
XLA Modules:
  0.0 91.8 jit_solution(4406899785674392635)
XLA Ops:
  0.0 0.0 copy-start.3
  0.0 0.0 copy-start.2
  0.0 0.0 copy-start.1
  0.0 9.4 %all-to-all-start = ((f32[16,64,256]{2,1,0:T(8,128)}), f32[16,64,256]{2,1,0:T(8,128)S(1)}, u32[]{:S(2)}, u32[]{:S(2)}) async-start(f32[16,64,256]{2,1,0:T(8,128)} %bitcast.91), calls=%async_computation | async-start | bytes 2097152 | tf_op jit(solution)/shard_map/all_to_all | solution.py:32
  9.4 0.0 copy-done.1
  9.5 0.1 select_reduce_fusion
  9.6 0.1 select_reduce_fusion.1
  9.7 0.2 convert_reduce_fusion.1
  9.9 0.1 fusion.1
  10.0 0.6 convert_reduce_fusion.2
  14.5 0.6 slice_reduce_fusion
  15.9 0.1 convert_reduce_fusion
  16.0 0.0 copy-done.3
  16.0 0.2 select_reduce_fusion.4
  16.2 0.0 copy-done.2
  16.2 0.2 select_reduce_fusion.2
  16.4 19.9 %all-to-all-done = f32[16,64,256]{2,1,0:T(8,128)S(1)} async-done(((f32[16,64,256]{2,1,0:T(8,128)}), f32[16,64,256]{2,1,0:T(8,128)S(1)}, u32[]{:S(2)}, u32[]{:S(2)}) %all-to-all-start) | async-done | bytes 1048608 | tf_op jit(solution)/shard_map/all_to_all | solution.py:32
  36.3 1.6 %conditional.1 = (f32[16,64,256]{2,1,0:T(8,128)}) conditional(s32[]{:T(128)} %clamp.3, (s32[16]{0:T(128)S(1)}, f32[16,64,256]{2,1,0:T(8,128)S(1)}) %tuple.44, (s32[16]{0:T(128)S(1)}, s32[16]{0:T(128)S(1)}, f32[16,64,256]{2,1,0:T(8,128)S(1)}) %tuple.45, (s32[16]{0:T(128)S(1)}, s32[16]{0:T(128)S(1)}, ...), branch_computations={%region_10.11_spmd, %region_11.12_spmd, %region_12.13_spmd, %regio... | conditional | flops 1575008 | bytes 12591408 | solution.py:84
  36.3 1.6 %gather_fusion = f32[16,64,256]{2,1,0:T(8,128)} fusion(f32[16,64,256]{2,1,0:T(8,128)S(1)} %get-tuple-element.81, s32[1024]{0:T(1024)S(1)} %pad_clamp_fusion), kind=kCustom, calls=%fused_computation | custom fusion | bytes 2097216 | tf_op jit(solution)/shard_map/cond/branch_0_fun/jit(_take)/gather | solution.py:68
  37.9 0.0 copy-start
  37.9 4.8 %all-to-all-start.1 = ((f32[16,64,256]{2,1,0:T(8,128)}), f32[16,64,256]{2,1,0:T(8,128)S(1)}, u32[]{:S(2)}, u32[]{:S(2)}) async-start(f32[16,64,256]{2,1,0:T(8,128)} %get-tuple-element.227), calls=%async_computation.1 | async-start | bytes 2097152 | tf_op jit(solution)/shard_map/all_to_all | solution.py:32
  42.7 26.6 %all-to-all-done.1 = f32[16,64,256]{2,1,0:T(8,128)S(1)} async-done(((f32[16,64,256]{2,1,0:T(8,128)}), f32[16,64,256]{2,1,0:T(8,128)S(1)}, u32[]{:S(2)}, u32[]{:S(2)}) %all-to-all-start.1) | async-done | bytes 1048608 | tf_op jit(solution)/shard_map/all_to_all | solution.py:32
  69.2 0.0 copy-done
  69.2 0.3 shard_map.55.refs_0_.sent
  69.6 1.9 %collective-permute-start.13 = (f32[2,256,256]{2,1,0:T(8,128)S(1)}, f32[2,256,256]{2,1,0:T(8,128)S(1)}, u32[]{:S(2)}, u32[]{:S(2)}) collective-permute-start(f32[2,256,256]{2,1,0:T(8,128)S(1)} %shard_map.55.refs_0_.sent), channel_id=1, source_target_pairs={{0,1},{1,0},{2,3},{3,2},{4,5},{5,4},{6,7},{7,6},{8,9},{9,8},{10,11... | collective-permute-start | bytes 1572872 | tf_op jit(solution)/shard_map/ppermute | solution.py:226
  71.5 0.4 shard_map.56.sent
  71.9 9.1 %collective-permute-start.12 = (f32[2,256,256]{2,1,0:T(8,128)S(1)}, f32[2,256,256]{2,1,0:T(8,128)S(1)}, u32[]{:S(2)}, u32[]{:S(2)}) collective-permute-start(f32[2,256,256]{2,1,0:T(8,128)S(1)} %shard_map.56.sent), channel_id=1, source_target_pairs={{0,15},{1,2},{2,1},{3,4},{4,3},{5,6},{6,5},{7,8},{8,7},{9,10},{10,... | collective-permute-start | bytes 1572872 | tf_op jit(solution)/shard_map/ppermute | solution.py:227
  81.1 0.0 collective-permute-done.13.first
  81.1 2.1 %shard_map.57 = (f32[2,256,256]{2,1,0:T(8,128)S(1)}, f32[4,256,256]{2,1,0:T(8,128)}) custom-call(s32[1]{0:T(128)} %bitcast.34.above.even, f32[4,256,256]{2,1,0:T(8,128)S(1)} %bitcast.90, f32[2,256,256]{2,1,0:T(8,128)S(1)} %shard_map.55.refs_0_.sent, f32[2,256,256]{2,1,0:T(8,128)S(1)} %collective-permute-done.13.first, f32[2,4,256,256]{3,2,1,0:T(8,128)S(1)} %bitcast.87), custom_call_target="tpu_custom_call" | custom-call | flops 5242880 | bytes 5242880 | tf_op jit(solution)/shard_map/pallas_call | solution.py:230
  83.3 7.4 %collective-permute-done.12.second = f32[2,256,256]{2,1,0:T(8,128)S(1)} collective-permute-done((f32[2,256,256]{2,1,0:T(8,128)S(1)}, f32[2,256,256]{2,1,0:T(8,128)S(1)}, u32[]{:S(2)}, u32[]{:S(2)}) %collective-permute-start.12) | collective-permute-done | bytes 524320 | tf_op jit(solution)/shard_map/ppermute | solution.py:227
  90.7 1.1 %shard_map.58 = f32[4,256,256]{2,1,0:T(8,128)} custom-call(s32[1]{0:T(128)} %bitcast.34.above.even, f32[2,256,256]{2,1,0:T(8,128)S(1)} %shard_map.56.sent, f32[2,256,256]{2,1,0:T(8,128)S(1)} %collective-permute-done.12.second, f32[2,256,256]{2,1,0:T(8,128)S(1)} %pad_maximum_fusion.2.kicks, ...), custom_call_target="tpu_custom_call", output_to_operand_aliasing={{}: (5, {})} | custom-call | flops 1048576 | bytes 2621440 | tf_op jit(solution)/shard_map/pallas_call | solution.py:240
  (10 shorter events, 0.1 us)
Async XLA Ops:
  0.0 16.0 %copy-start.3 = (s32[16]{0:T(128)S(1)}, s32[16]{0:T(128)}, u32[]{:S(2)}) copy-start(s32[16]{0:T(128)} %constant.147.clone) | copy-start | bytes 196
  0.0 16.2 %copy-start.2 = (s32[32]{0:T(128)S(1)}, s32[32]{0:T(128)}, u32[]{:S(2)}) copy-start(s32[32]{0:T(128)} %constant.146.clone) | copy-start | bytes 388
  0.0 9.4 %copy-start.1 = (s32[32]{0:T(128)S(1)}, s32[32]{0:T(128)}, u32[]{:S(2)}) copy-start(s32[32]{0:T(128)} %param.19) | copy-start | bytes 388
  0.0 36.3 %all-to-all-start = ((f32[16,64,256]{2,1,0:T(8,128)}), f32[16,64,256]{2,1,0:T(8,128)S(1)}, u32[]{:S(2)}, u32[]{:S(2)}) async-start(f32[16,64,256]{2,1,0:T(8,128)} %bitcast.91), calls=%async_computation | async-start | bytes 2097152 | tf_op jit(solution)/shard_map/all_to_all | solution.py:32
  37.9 31.4 %copy-start = (f32[2,1,4,256,256]{4,3,2,1,0:T(8,128)S(1)}, f32[2,1,4,256,256]{4,3,2,1,0:T(8,128)}, u32[]{:S(2)}) copy-start(f32[2,1,4,256,256]{4,3,2,1,0:T(8,128)} %param.20) | copy-start | bytes 6291460
  37.9 31.4 %all-to-all-start.1 = ((f32[16,64,256]{2,1,0:T(8,128)}), f32[16,64,256]{2,1,0:T(8,128)S(1)}, u32[]{:S(2)}, u32[]{:S(2)}) async-start(f32[16,64,256]{2,1,0:T(8,128)} %get-tuple-element.227), calls=%async_computation.1 | async-start | bytes 2097152 | tf_op jit(solution)/shard_map/all_to_all | solution.py:32
  69.6 11.5 %collective-permute-start.13 = (f32[2,256,256]{2,1,0:T(8,128)S(1)}, f32[2,256,256]{2,1,0:T(8,128)S(1)}, u32[]{:S(2)}, u32[]{:S(2)}) collective-permute-start(f32[2,256,256]{2,1,0:T(8,128)S(1)} %shard_map.55.refs_0_.sent), channel_id=1, source_target_pairs={{0,1},{1,0},{2,3},{3,2},{4,5},{5,4},{6,7},{7,6},{8,9},{9,8},{10,11... | collective-permute-start | bytes 1572872 | tf_op jit(solution)/shard_map/ppermute | solution.py:226
  71.9 18.8 %collective-permute-start.12 = (f32[2,256,256]{2,1,0:T(8,128)S(1)}, f32[2,256,256]{2,1,0:T(8,128)S(1)}, u32[]{:S(2)}, u32[]{:S(2)}) collective-permute-start(f32[2,256,256]{2,1,0:T(8,128)S(1)} %shard_map.56.sent), channel_id=1, source_target_pairs={{0,15},{1,2},{2,1},{3,4},{4,3},{5,6},{6,5},{7,8},{8,7},{9,10},{10,... | collective-permute-start | bytes 1572872 | tf_op jit(solution)/shard_map/ppermute | solution.py:227

commit v7 on v6

--- a/solution.py
+++ b/solution.py
@@ -12,7 +12,7 @@
 COUPLING = 0.5
 KICK = (2.0 * STEP_SIZE) ** 0.5
 HALF = 16
-STRIP = 128
+STRIP = 256
 VMEM = pl.BlockSpec(memory_space=pltpu.VMEM)
 SMEM = pl.BlockSpec(memory_space=pltpu.SMEM)
 HBM = pl.BlockSpec(memory_space=pl.ANY)

time: 92.2 us -> 109 us (1.18)
  the two profiles are of different devices: /device:TPU:8 before, /device:TPU:78 now
where the time goes in v7:
time: 109 us
  waiting for transfers between devices  67 us (61%)
  starting transfers between devices  28.6 us (26%)
  between operations  4.72 us (4%)
  other arithmetic  3.66 us (3%)
  Pallas kernels  3.55 us (3%)
  local copies, waits for them, and re-layouts  1.25 us (1%)
    all_to_all x2, waiting for transfers between devices, exchange(): lax.all_to_all(parts, 'rep', split_axis=0, concat_axis=0, tiled=True, axi...  46.2 us
    all_to_all x2, starting transfers between devices, exchange(): lax.all_to_all(parts, 'rep', split_axis=0, concat_axis=0, tiled=True, axi...  11.9 us
    ppermute x1, waiting for transfers between devices, crossing(): lax.ppermute(jnp.take(spread, send[:width], axis=0, mode='clip'), 'rep',...  11.4 us
    ppermute x1, starting transfers between devices, crossing(): lax.ppermute(jnp.take(spread, send[:width], axis=0, mode='clip'), 'rep',...  10 us
    ppermute x1, waiting for transfers between devices, shards(): first = lax.ppermute(inner, ('rep', 'slab'), side_swap(0, size))  6.52 us
    ppermute x1, starting transfers between devices, shards(): second = lax.ppermute(outer, ('rep', 'slab'), side_swap(1, size))  3.93 us
    ppermute x1, waiting for transfers between devices, shards(): second = lax.ppermute(outer, ('rep', 'slab'), side_swap(1, size))  2.97 us
    ppermute x1, starting transfers between devices, shards(): first = lax.ppermute(inner, ('rep', 'slab'), side_swap(0, size))  2.74 us
  transfers between devices with their start and end apart: 5, of which 5 were waited for; matrix products, arithmetic and copies ran while one was open for 3% of the time, Pallas kernels for 2%

profile of v7, /device:TPU:78, one launch (start us, length us, event | category | flops | bytes accessed | tf_op | source)
XLA Modules:
  0.0 108.8 jit_solution(4777695861192586150)
XLA Ops:
  0.0 0.0 copy-start.3
  0.0 7.7 %all-to-all-start = ((f32[16,64,256]{2,1,0:T(8,128)}), f32[16,64,256]{2,1,0:T(8,128)S(1)}, u32[]{:S(2)}, u32[]{:S(2)}) async-start(f32[16,64,256]{2,1,0:T(8,128)} %bitcast.91), calls=%async_computation | async-start | bytes 2097152 | tf_op jit(solution)/shard_map/all_to_all | solution.py:32
  7.7 0.0 copy-done.1
  7.7 0.1 select_reduce_fusion
  7.9 0.1 select_reduce_fusion.1
  8.0 0.2 convert_reduce_fusion.1
  8.2 0.1 fusion.1
  8.3 0.6 convert_reduce_fusion.2
  12.8 0.6 slice_reduce_fusion
  14.1 0.1 convert_reduce_fusion
  14.2 0.0 copy-done.3
  14.3 0.2 select_reduce_fusion.4
  14.5 0.0 copy-done.2
  14.5 0.2 select_reduce_fusion.2
  14.7 19.6 %all-to-all-done = f32[16,64,256]{2,1,0:T(8,128)S(1)} async-done(((f32[16,64,256]{2,1,0:T(8,128)}), f32[16,64,256]{2,1,0:T(8,128)S(1)}, u32[]{:S(2)}, u32[]{:S(2)}) %all-to-all-start) | async-done | bytes 1048608 | tf_op jit(solution)/shard_map/all_to_all | solution.py:32
  34.3 24.0 %conditional.1 = (f32[16,64,256]{2,1,0:T(8,128)}) conditional(s32[]{:T(128)} %clamp.3, (s32[16]{0:T(128)S(1)}, f32[16,64,256]{2,1,0:T(8,128)S(1)}) %tuple.44, (s32[16]{0:T(128)S(1)}, s32[16]{0:T(128)S(1)}, f32[16,64,256]{2,1,0:T(8,128)S(1)}) %tuple.45, (s32[16]{0:T(128)S(1)}, s32[16]{0:T(128)S(1)}, ...), branch_computations={%region_10.11_spmd, %region_11.12_spmd, %region_12.13_spmd, %regio... | conditional | flops 1575008 | bytes 12591408 | solution.py:84
  34.3 0.6 gather_fusion.5
  34.9 10.0 %collective-permute-start.2 = (f32[4,64,256]{2,1,0:T(8,128)S(1)}, f32[4,64,256]{2,1,0:T(8,128)S(1)}, u32[]{:S(2)}, u32[]{:S(2)}) collective-permute-start(f32[4,64,256]{2,1,0:T(8,128)S(1)} %gather_fusion.5), channel_id=1, source_target_pairs={{0,256},{16,272},{32,288},{48,304},{64,320},{80,336},{96,352},{112... | collective-permute-start | bytes 786440 | tf_op jit(solution)/shard_map/cond/branch_4_fun/ppermute | solution.py:72
  44.9 0.6 gather_fusion.6
  45.6 11.4 %collective-permute-done.2 = f32[4,64,256]{2,1,0:T(8,128)S(1)} collective-permute-done((f32[4,64,256]{2,1,0:T(8,128)S(1)}, f32[4,64,256]{2,1,0:T(8,128)S(1)}, u32[]{:S(2)}, u32[]{:S(2)}) %collective-permute-start.2) | collective-permute-done | bytes 262176 | tf_op jit(solution)/shard_map/cond/branch_4_fun/ppermute | solution.py:72
  56.9 1.3 %select_select_fusion.2 = f32[16,64,256]{2,1,0:T(8,128)} fusion(f32[16,64,256]{2,1,0:T(8,128)S(1)} %gather_fusion.6, f32[64,256]{1,0:T(8,128)S(1)} %get-tuple-element.172, f32[64,256]{1,0:T(8,128)S(1)} %get-tuple-element.173, f32[64,256]{1,0:T(8,128)S(1)} %get-tuple-element.174, f32[64,256]{1,0:T(8,128)S(1)} %get-tuple-element.171, ...), kind=kLoop, calls=%fused_computation.40 | loop fusion | flops 1048576 | bytes 2359360 | tf_op jit(solution)/shard_map/cond/branch_4_fun/jit(_where)/select_n | solution.py:77
  58.2 4.2 %all-to-all-start.1 = ((f32[16,64,256]{2,1,0:T(8,128)}), f32[16,64,256]{2,1,0:T(8,128)S(1)}, u32[]{:S(2)}, u32[]{:S(2)}) async-start(f32[16,64,256]{2,1,0:T(8,128)} %get-tuple-element.227), calls=%async_computation.1 | async-start | bytes 2097152 | tf_op jit(solution)/shard_map/all_to_all | solution.py:32
  62.4 26.6 %all-to-all-done.1 = f32[16,64,256]{2,1,0:T(8,128)S(1)} async-done(((f32[16,64,256]{2,1,0:T(8,128)}), f32[16,64,256]{2,1,0:T(8,128)S(1)}, u32[]{:S(2)}, u32[]{:S(2)}) %all-to-all-start.1) | async-done | bytes 1048608 | tf_op jit(solution)/shard_map/all_to_all | solution.py:32
  89.0 0.0 copy-done
  89.0 0.3 shard_map.55.refs_0_.sent
  89.2 2.7 %collective-permute-start.13 = (f32[2,256,256]{2,1,0:T(8,128)S(1)}, f32[2,256,256]{2,1,0:T(8,128)S(1)}, u32[]{:S(2)}, u32[]{:S(2)}) collective-permute-start(f32[2,256,256]{2,1,0:T(8,128)S(1)} %shard_map.55.refs_0_.sent), channel_id=1, source_target_pairs={{0,1},{1,0},{2,3},{3,2},{4,5},{5,4},{6,7},{7,6},{8,9},{9,8},{10,11... | collective-permute-start | bytes 1572872 | tf_op jit(solution)/shard_map/ppermute | solution.py:226
  92.0 0.3 shard_map.56.sent
  92.3 3.9 %collective-permute-start.12 = (f32[2,256,256]{2,1,0:T(8,128)S(1)}, f32[2,256,256]{2,1,0:T(8,128)S(1)}, u32[]{:S(2)}, u32[]{:S(2)}) collective-permute-start(f32[2,256,256]{2,1,0:T(8,128)S(1)} %shard_map.56.sent), channel_id=1, source_target_pairs={{0,15},{1,2},{2,1},{3,4},{4,3},{5,6},{6,5},{7,8},{8,7},{9,10},{10,... | collective-permute-start | bytes 1572872 | tf_op jit(solution)/shard_map/ppermute | solution.py:227
  96.3 6.5 %collective-permute-done.13.first = f32[2,256,256]{2,1,0:T(8,128)S(1)} collective-permute-done((f32[2,256,256]{2,1,0:T(8,128)S(1)}, f32[2,256,256]{2,1,0:T(8,128)S(1)}, u32[]{:S(2)}, u32[]{:S(2)}) %collective-permute-start.13) | collective-permute-done | bytes 524320 | tf_op jit(solution)/shard_map/ppermute | solution.py:226
  102.8 2.0 %shard_map.57 = (f32[2,256,256]{2,1,0:T(8,128)S(1)}, f32[4,256,256]{2,1,0:T(8,128)}) custom-call(s32[1]{0:T(128)} %bitcast.34.above.even, f32[4,256,256]{2,1,0:T(8,128)S(1)} %bitcast.90, f32[2,256,256]{2,1,0:T(8,128)S(1)} %shard_map.55.refs_0_.sent, f32[2,256,256]{2,1,0:T(8,128)S(1)} %collective-permute-done.13.first, f32[2,4,256,256]{3,2,1,0:T(8,128)S(1)} %bitcast.87), custom_call_target="tpu_custom_call" | custom-call | flops 5242880 | bytes 5242880 | tf_op jit(solution)/shard_map/pallas_call | solution.py:230
  104.8 3.0 %collective-permute-done.12.second = f32[2,256,256]{2,1,0:T(8,128)S(1)} collective-permute-done((f32[2,256,256]{2,1,0:T(8,128)S(1)}, f32[2,256,256]{2,1,0:T(8,128)S(1)}, u32[]{:S(2)}, u32[]{:S(2)}) %collective-permute-start.12) | collective-permute-done | bytes 524320 | tf_op jit(solution)/shard_map/ppermute | solution.py:227
  107.8 1.0 shard_map.58
  (16 shorter events, 0.2 us)
Async XLA Ops:
  0.0 14.2 %copy-start.3 = (s32[16]{0:T(128)S(1)}, s32[16]{0:T(128)}, u32[]{:S(2)}) copy-start(s32[16]{0:T(128)} %constant.147.clone) | copy-start | bytes 196
  0.0 14.5 %copy-start.2 = (s32[32]{0:T(128)S(1)}, s32[32]{0:T(128)}, u32[]{:S(2)}) copy-start(s32[32]{0:T(128)} %constant.146.clone) | copy-start | bytes 388
  0.0 7.7 %copy-start.1 = (s32[32]{0:T(128)S(1)}, s32[32]{0:T(128)}, u32[]{:S(2)}) copy-start(s32[32]{0:T(128)} %param.19) | copy-start | bytes 388
  0.0 34.3 %all-to-all-start = ((f32[16,64,256]{2,1,0:T(8,128)}), f32[16,64,256]{2,1,0:T(8,128)S(1)}, u32[]{:S(2)}, u32[]{:S(2)}) async-start(f32[16,64,256]{2,1,0:T(8,128)} %bitcast.91), calls=%async_computation | async-start | bytes 2097152 | tf_op jit(solution)/shard_map/all_to_all | solution.py:32
  34.9 22.0 %collective-permute-start.2 = (f32[4,64,256]{2,1,0:T(8,128)S(1)}, f32[4,64,256]{2,1,0:T(8,128)S(1)}, u32[]{:S(2)}, u32[]{:S(2)}) collective-permute-start(f32[4,64,256]{2,1,0:T(8,128)S(1)} %gather_fusion.5), channel_id=1, source_target_pairs={{0,256},{16,272},{32,288},{48,304},{64,320},{80,336},{96,352},{112... | collective-permute-start | bytes 786440 | tf_op jit(solution)/shard_map/cond/branch_4_fun/ppermute | solution.py:72
  58.2 30.7 %copy-start = (f32[2,1,4,256,256]{4,3,2,1,0:T(8,128)S(1)}, f32[2,1,4,256,256]{4,3,2,1,0:T(8,128)}, u32[]{:S(2)}) copy-start(f32[2,1,4,256,256]{4,3,2,1,0:T(8,128)} %param.20) | copy-start | bytes 6291460
  58.2 30.7 %all-to-all-start.1 = ((f32[16,64,256]{2,1,0:T(8,128)}), f32[16,64,256]{2,1,0:T(8,128)S(1)}, u32[]{:S(2)}, u32[]{:S(2)}) async-start(f32[16,64,256]{2,1,0:T(8,128)} %get-tuple-element.227), calls=%async_computation.1 | async-start | bytes 2097152 | tf_op jit(solution)/shard_map/all_to_all | solution.py:32
  89.2 13.6 %collective-permute-start.13 = (f32[2,256,256]{2,1,0:T(8,128)S(1)}, f32[2,256,256]{2,1,0:T(8,128)S(1)}, u32[]{:S(2)}, u32[]{:S(2)}) collective-permute-start(f32[2,256,256]{2,1,0:T(8,128)S(1)} %shard_map.55.refs_0_.sent), channel_id=1, source_target_pairs={{0,1},{1,0},{2,3},{3,2},{4,5},{5,4},{6,7},{7,6},{8,9},{9,8},{10,11... | collective-permute-start | bytes 1572872 | tf_op jit(solution)/shard_map/ppermute | solution.py:226
  92.3 15.5 %collective-permute-start.12 = (f32[2,256,256]{2,1,0:T(8,128)S(1)}, f32[2,256,256]{2,1,0:T(8,128)S(1)}, u32[]{:S(2)}, u32[]{:S(2)}) collective-permute-start(f32[2,256,256]{2,1,0:T(8,128)S(1)} %shard_map.56.sent), channel_id=1, source_target_pairs={{0,15},{1,2},{2,1},{3,4},{4,3},{5,6},{6,5},{7,8},{8,7},{9,10},{10,... | collective-permute-start | bytes 1572872 | tf_op jit(solution)/shard_map/ppermute | solution.py:227

commit v8 on v6

--- a/solution.py
+++ b/solution.py
@@ -24,7 +24,7 @@
 
 
 def ring_order():
-    return [((3 * y) % 8) * 2 + core for y in range(8) for core in range(2)]
+    return [(3 * y % 8) * 2 for y in range(8)] + [y * 2 + 1 for y in range(8)]
 
 
 def exchange(parts, order):

time: 92.2 us -> 103 us (1.12)
  starting transfers between devices: 25.3 us -> 33.5 us
  waiting for transfers between devices: 53.9 us -> 56.7 us
  other arithmetic: 2.34 us -> 3.53 us
    ppermute x0 -> x1, starting transfers between devices: none -> 9.44 us  [crossing(): lax.ppermute(jnp.take(spread, send[:width], axis=0, mode='clip'), 'rep',...]
    ppermute x0 -> x1, waiting for transfers between devices: none -> 2.86 us  [crossing(): lax.ppermute(jnp.take(spread, send[:width], axis=0, mode='clip'), 'rep',...]
    ppermute x1, starting transfers between devices: 9.15 us -> 6.74 us  [shards(): second = lax.ppermute(outer, ('rep', 'slab'), side_swap(1, size))]
    ppermute x1, starting transfers between devices: 1.92 us -> 3.39 us  [shards(): first = lax.ppermute(inner, ('rep', 'slab'), side_swap(0, size))]
    select_n x0 -> x1, other arithmetic: none -> 1.17 us  [crossing(): parts = jnp.where((pick == HALF + i)[:, None, None], far[i:i + 1], parts)]
  transfers between devices with their start and end apart: 4 -> 5, of which waited for: 3 -> 5; matrix products, arithmetic and copies ran while one was open for 3% -> 3% of each run, Pallas kernels for 3% -> 2%
where the time goes in v8:
time: 103 us; the launch traced here: 104 us
  waiting for transfers between devices  56.7 us (55%)
  starting transfers between devices  33.5 us (33%)
  between operations  4.72 us (5%)
  Pallas kernels  3.95 us (4%)
  other arithmetic  3.53 us (3%)
  local copies, waits for them, and re-layouts  1.23 us (1%)
    all_to_all x2, waiting for transfers between devices, exchange(): lax.all_to_all(parts, 'rep', split_axis=0, concat_axis=0, tiled=True, axi...  45.5 us
    all_to_all x2, starting transfers between devices, exchange(): lax.all_to_all(parts, 'rep', split_axis=0, concat_axis=0, tiled=True, axi...  13.9 us
    ppermute x1, starting transfers between devices, crossing(): lax.ppermute(jnp.take(spread, send[:width], axis=0, mode='clip'), 'rep',...  9.44 us
    ppermute x1, waiting for transfers between devices, shards(): second = lax.ppermute(outer, ('rep', 'slab'), side_swap(1, size))  7.82 us
    ppermute x1, starting transfers between devices, shards(): second = lax.ppermute(outer, ('rep', 'slab'), side_swap(1, size))  6.74 us
    ppermute x1, starting transfers between devices, shards(): first = lax.ppermute(inner, ('rep', 'slab'), side_swap(0, size))  3.39 us
    ppermute x1, waiting for transfers between devices, crossing(): lax.ppermute(jnp.take(spread, send[:width], axis=0, mode='clip'), 'rep',...  2.86 us
    pallas_call x1, Pallas kernels, shards(): pl.pallas_call(near_kernel, out_shape=[pair, result], in_specs=[SMEM] + [...  2.12 us
  transfers between devices with their start and end apart: 5, of which 5 were waited for; matrix products, arithmetic and copies ran while one was open for 3% of the time, Pallas kernels for 2%

profile of v8, /device:TPU:8, one launch (start us, length us, event | category | flops | bytes accessed | tf_op | source)
XLA Modules:
  0.0 103.6 jit_solution(9049126845862354668)
XLA Ops:
  0.0 0.0 copy-start.3
  0.0 9.4 %all-to-all-start = ((f32[16,64,256]{2,1,0:T(8,128)}), f32[16,64,256]{2,1,0:T(8,128)S(1)}, u32[]{:S(2)}, u32[]{:S(2)}) async-start(f32[16,64,256]{2,1,0:T(8,128)} %bitcast.91), calls=%async_computation | async-start | bytes 2097152 | tf_op jit(solution)/shard_map/all_to_all | solution.py:32
  9.4 0.0 copy-done.1
  9.4 0.1 select_reduce_fusion
  9.6 0.1 select_reduce_fusion.1
  9.7 0.2 convert_reduce_fusion.1
  9.9 0.1 fusion.1
  10.0 0.6 convert_reduce_fusion.2
  14.5 0.6 slice_reduce_fusion
  15.8 0.1 convert_reduce_fusion
  15.9 0.0 copy-done.3
  16.0 0.2 select_reduce_fusion.4
  16.2 0.0 copy-done.2
  16.2 0.2 select_reduce_fusion.2
  16.4 19.2 %all-to-all-done = f32[16,64,256]{2,1,0:T(8,128)S(1)} async-done(((f32[16,64,256]{2,1,0:T(8,128)}), f32[16,64,256]{2,1,0:T(8,128)S(1)}, u32[]{:S(2)}, u32[]{:S(2)}) %all-to-all-start) | async-done | bytes 1048608 | tf_op jit(solution)/shard_map/all_to_all | solution.py:32
  35.6 14.7 %conditional.1 = (f32[16,64,256]{2,1,0:T(8,128)}) conditional(s32[]{:T(128)} %clamp.3, (s32[16]{0:T(128)S(1)}, f32[16,64,256]{2,1,0:T(8,128)S(1)}) %tuple.44, (s32[16]{0:T(128)S(1)}, s32[16]{0:T(128)S(1)}, f32[16,64,256]{2,1,0:T(8,128)S(1)}) %tuple.45, (s32[16]{0:T(128)S(1)}, s32[16]{0:T(128)S(1)}, ...), branch_computations={%region_10.11_spmd, %region_11.12_spmd, %region_12.13_spmd, %regio... | conditional | flops 1575008 | bytes 12591408 | solution.py:84
  35.6 0.6 gather_fusion.1
  36.1 9.4 %collective-permute-start = (f32[2,64,256]{2,1,0:T(8,128)S(1)}, f32[2,64,256]{2,1,0:T(8,128)S(1)}, u32[]{:S(2)}, u32[]{:S(2)}) collective-permute-start(f32[2,64,256]{2,1,0:T(8,128)S(1)} %gather_fusion.1), channel_id=1, source_target_pairs={{0,256},{16,272},{32,288},{48,304},{64,320},{80,336},{96,352},{112... | collective-permute-start | bytes 393224 | tf_op jit(solution)/shard_map/cond/branch_2_fun/ppermute | solution.py:72
  45.6 0.6 gather_fusion.2
  46.2 2.9 %collective-permute-done = f32[2,64,256]{2,1,0:T(8,128)S(1)} collective-permute-done((f32[2,64,256]{2,1,0:T(8,128)S(1)}, f32[2,64,256]{2,1,0:T(8,128)S(1)}, u32[]{:S(2)}, u32[]{:S(2)}) %collective-permute-start) | collective-permute-done | bytes 131104 | tf_op jit(solution)/shard_map/cond/branch_2_fun/ppermute | solution.py:72
  49.1 1.2 %select_select_fusion = f32[16,64,256]{2,1,0:T(8,128)} fusion(f32[16,64,256]{2,1,0:T(8,128)S(1)} %gather_fusion.2, f32[64,256]{1,0:T(8,128)S(1)} %get-tuple-element.162, f32[64,256]{1,0:T(8,128)S(1)} %get-tuple-element.161, pred[16]{0:T(512)(128)(4,1)S(1)} %get-tuple-element.164, pred[16]{0:T(512)(128)(4,1)S(1)} %get-tuple-element.163), kind=kLoop, calls=%fused_computation.24 | loop fusion | flops 524288 | bytes 2228256 | tf_op jit(solution)/shard_map/cond/branch_2_fun/jit(_where)/select_n | solution.py:77
  50.3 4.5 %all-to-all-start.1 = ((f32[16,64,256]{2,1,0:T(8,128)}), f32[16,64,256]{2,1,0:T(8,128)S(1)}, u32[]{:S(2)}, u32[]{:S(2)}) async-start(f32[16,64,256]{2,1,0:T(8,128)} %get-tuple-element.227), calls=%async_computation.1 | async-start | bytes 2097152 | tf_op jit(solution)/shard_map/all_to_all | solution.py:32
  54.7 26.4 %all-to-all-done.1 = f32[16,64,256]{2,1,0:T(8,128)S(1)} async-done(((f32[16,64,256]{2,1,0:T(8,128)}), f32[16,64,256]{2,1,0:T(8,128)S(1)}, u32[]{:S(2)}, u32[]{:S(2)}) %all-to-all-start.1) | async-done | bytes 1048608 | tf_op jit(solution)/shard_map/all_to_all | solution.py:32
  81.1 0.0 copy-done
  81.1 0.3 shard_map.55.refs_0_.sent
  81.5 3.4 %collective-permute-start.13 = (f32[2,256,256]{2,1,0:T(8,128)S(1)}, f32[2,256,256]{2,1,0:T(8,128)S(1)}, u32[]{:S(2)}, u32[]{:S(2)}) collective-permute-start(f32[2,256,256]{2,1,0:T(8,128)S(1)} %shard_map.55.refs_0_.sent), channel_id=1, source_target_pairs={{0,1},{1,0},{2,3},{3,2},{4,5},{5,4},{6,7},{7,6},{8,9},{9,8},{10,11... | collective-permute-start | bytes 1572872 | tf_op jit(solution)/shard_map/ppermute | solution.py:226
  84.9 0.4 shard_map.56.sent
  85.2 6.7 %collective-permute-start.12 = (f32[2,256,256]{2,1,0:T(8,128)S(1)}, f32[2,256,256]{2,1,0:T(8,128)S(1)}, u32[]{:S(2)}, u32[]{:S(2)}) collective-permute-start(f32[2,256,256]{2,1,0:T(8,128)S(1)} %shard_map.56.sent), channel_id=1, source_target_pairs={{0,15},{1,2},{2,1},{3,4},{4,3},{5,6},{6,5},{7,8},{8,7},{9,10},{10,... | collective-permute-start | bytes 1572872 | tf_op jit(solution)/shard_map/ppermute | solution.py:227
  92.1 0.5 collective-permute-done.13.first
  92.5 2.1 %shard_map.57 = (f32[2,256,256]{2,1,0:T(8,128)S(1)}, f32[4,256,256]{2,1,0:T(8,128)}) custom-call(s32[1]{0:T(128)} %bitcast.34.above.even, f32[4,256,256]{2,1,0:T(8,128)S(1)} %bitcast.90, f32[2,256,256]{2,1,0:T(8,128)S(1)} %shard_map.55.refs_0_.sent, f32[2,256,256]{2,1,0:T(8,128)S(1)} %collective-permute-done.13.first, f32[2,4,256,256]{3,2,1,0:T(8,128)S(1)} %bitcast.87), custom_call_target="tpu_custom_call" | custom-call | flops 5242880 | bytes 5242880 | tf_op jit(solution)/shard_map/pallas_call | solution.py:230
  94.7 7.8 %collective-permute-done.12.second = f32[2,256,256]{2,1,0:T(8,128)S(1)} collective-permute-done((f32[2,256,256]{2,1,0:T(8,128)S(1)}, f32[2,256,256]{2,1,0:T(8,128)S(1)}, u32[]{:S(2)}, u32[]{:S(2)}) %collective-permute-start.12) | collective-permute-done | bytes 524320 | tf_op jit(solution)/shard_map/ppermute | solution.py:227
  102.5 1.1 %shard_map.58 = f32[4,256,256]{2,1,0:T(8,128)} custom-call(s32[1]{0:T(128)} %bitcast.34.above.even, f32[2,256,256]{2,1,0:T(8,128)S(1)} %shard_map.56.sent, f32[2,256,256]{2,1,0:T(8,128)S(1)} %collective-permute-done.12.second, f32[2,256,256]{2,1,0:T(8,128)S(1)} %pad_maximum_fusion.2.kicks, ...), custom_call_target="tpu_custom_call", output_to_operand_aliasing={{}: (5, {})} | custom-call | flops 1048576 | bytes 2621440 | tf_op jit(solution)/shard_map/pallas_call | solution.py:240
  (16 shorter events, 0.2 us)
Async XLA Ops:
  0.0 15.9 %copy-start.3 = (s32[16]{0:T(128)S(1)}, s32[16]{0:T(128)}, u32[]{:S(2)}) copy-start(s32[16]{0:T(128)} %constant.147.clone) | copy-start | bytes 196
  0.0 16.2 %copy-start.2 = (s32[32]{0:T(128)S(1)}, s32[32]{0:T(128)}, u32[]{:S(2)}) copy-start(s32[32]{0:T(128)} %constant.146.clone) | copy-start | bytes 388
  0.0 9.4 %copy-start.1 = (s32[32]{0:T(128)S(1)}, s32[32]{0:T(128)}, u32[]{:S(2)}) copy-start(s32[32]{0:T(128)} %param.19) | copy-start | bytes 388
  0.0 35.6 %all-to-all-start = ((f32[16,64,256]{2,1,0:T(8,128)}), f32[16,64,256]{2,1,0:T(8,128)S(1)}, u32[]{:S(2)}, u32[]{:S(2)}) async-start(f32[16,64,256]{2,1,0:T(8,128)} %bitcast.91), calls=%async_computation | async-start | bytes 2097152 | tf_op jit(solution)/shard_map/all_to_all | solution.py:32
  36.1 13.0 %collective-permute-start = (f32[2,64,256]{2,1,0:T(8,128)S(1)}, f32[2,64,256]{2,1,0:T(8,128)S(1)}, u32[]{:S(2)}, u32[]{:S(2)}) collective-permute-start(f32[2,64,256]{2,1,0:T(8,128)S(1)} %gather_fusion.1), channel_id=1, source_target_pairs={{0,256},{16,272},{32,288},{48,304},{64,320},{80,336},{96,352},{112... | collective-permute-start | bytes 393224 | tf_op jit(solution)/shard_map/cond/branch_2_fun/ppermute | solution.py:72
  50.3 30.8 %copy-start = (f32[2,1,4,256,256]{4,3,2,1,0:T(8,128)S(1)}, f32[2,1,4,256,256]{4,3,2,1,0:T(8,128)}, u32[]{:S(2)}) copy-start(f32[2,1,4,256,256]{4,3,2,1,0:T(8,128)} %param.20) | copy-start | bytes 6291460
  50.3 30.8 %all-to-all-start.1 = ((f32[16,64,256]{2,1,0:T(8,128)}), f32[16,64,256]{2,1,0:T(8,128)S(1)}, u32[]{:S(2)}, u32[]{:S(2)}) async-start(f32[16,64,256]{2,1,0:T(8,128)} %get-tuple-element.227), calls=%async_computation.1 | async-start | bytes 2097152 | tf_op jit(solution)/shard_map/all_to_all | solution.py:32
  81.5 11.1 %collective-permute-start.13 = (f32[2,256,256]{2,1,0:T(8,128)S(1)}, f32[2,256,256]{2,1,0:T(8,128)S(1)}, u32[]{:S(2)}, u32[]{:S(2)}) collective-permute-start(f32[2,256,256]{2,1,0:T(8,128)S(1)} %shard_map.55.refs_0_.sent), channel_id=1, source_target_pairs={{0,1},{1,0},{2,3},{3,2},{4,5},{5,4},{6,7},{7,6},{8,9},{9,8},{10,11... | collective-permute-start | bytes 1572872 | tf_op jit(solution)/shard_map/ppermute | solution.py:226
  85.2 17.3 %collective-permute-start.12 = (f32[2,256,256]{2,1,0:T(8,128)S(1)}, f32[2,256,256]{2,1,0:T(8,128)S(1)}, u32[]{:S(2)}, u32[]{:S(2)}) collective-permute-start(f32[2,256,256]{2,1,0:T(8,128)S(1)} %shard_map.56.sent), channel_id=1, source_target_pairs={{0,15},{1,2},{2,1},{3,4},{4,3},{5,6},{6,5},{7,8},{8,7},{9,10},{10,... | collective-permute-start | bytes 1572872 | tf_op jit(solution)/shard_map/ppermute | solution.py:227
